TPU v7x, 32 devices: a whole 2x2x4 slice. The times are simulated.
32 devices in a mesh: pipe: 2 (over x), dp: 4 (over y, core), tensor: 4 (over z).
Axes of the slice: x: 2, y: 2, z: 4, core: 2. Of those that a mesh axis runs over, the one named last changes fastest.
Arguments:
- section_rows: bfloat16 [2, 8, 2, 256, 768], P('pipe', 'dp', None, 'tensor'), may hold values from -6 to 6
- enc_lengths: int32 [8, 6], P('dp'), may hold values from 1 to 256, 512 in all within a row
- dec_lengths: int32 [8, 6], P('dp'), may hold values from 1 to 114, 256 in all within a row
- enc_buckets: int32 [1023], replicated, may hold values from 0 to 31
- dec_buckets: int32 [256], replicated, may hold values from 0 to 31
- norm_gains: float32 [2, 3, 768], P('pipe'), may hold values from 0.5 to 1.5
- rel_bias: float32 [2, 32, 12], P('pipe', None, 'tensor'), may hold values from -3 to 3
- query_key_w: bfloat16 [2, 2, 768, 768], P('pipe', None, 'dp', 'tensor'), may hold values from -0.078125 to 0.078125
- value_w: bfloat16 [2, 768, 768], P('pipe', 'dp', 'tensor'), may hold values from -0.21875 to 0.21875
- attn_out_w: bfloat16 [2, 768, 768], P('pipe', 'tensor', 'dp'), may hold values from -1 to 1
- cross_first: bfloat16 [2, 768, 768], P('pipe', 'dp', 'tensor'), may hold values from -0.078125 to 0.078125
- cross_second: bfloat16 [2, 768, 768], P('pipe', 'dp', 'tensor'), may hold values from -0.5 to 0.5
- ff_in: bfloat16 [2, 768, 3072], P('pipe', 'dp', 'tensor'), may hold values from -0.21875 to 0.21875
- ff_out: bfloat16 [2, 3072, 768], P('pipe', 'tensor', 'dp'), may hold values from -0.109375 to 0.109375
Outputs:
- section_out: float32 [2, 8, 2, 256, 768], P('pipe', 'dp', None, 'tensor')
- gain_grads: float32 [2, 3, 768], P('pipe', None, 'dp')
- bias_grads: float32 [2, 32, 12], P('pipe', 'dp', 'tensor')
- pair_grads: float32 [2, 2, 768, 768], P('pipe', None, 'dp', 'tensor')
- value_grads: float32 [2, 768, 768], P('pipe', 'dp', 'tensor')
- out_grads: float32 [2, 768, 768], P('pipe', 'tensor', 'dp')
- first_grads: float32 [2, 768, 768], P('pipe', 'dp', 'tensor')
- second_grads: float32 [2, 768, 768], P('pipe', 'dp', 'tensor')
- inner_grads: float32 [2, 768, 3072], P('pipe', 'dp', 'tensor')
- outer_grads: float32 [2, 3072, 768], P('pipe', 'tensor', 'dp')
Inputs may be any that keep to these rules, and one draw needn't show every extreme that they name: `enc_lengths`: each row's 6 lengths sum to 512; one of them is exactly 256. `dec_lengths`: each row's 6 lengths sum to 256; one of them is exactly 114.
All inputs are finite; a program needn't handle non-finite values.
Results may differ from a plain program's by a relative error of at most 0.025.
Values may be sent and summed in bfloat16 or wider, within the bound.
A program may use at most 192 MiB of HBM per device.

v0:
```python
import functools
import types

import jax
import jax.numpy as jnp
from jax import lax
from jax.experimental import pallas as pl
from jax.experimental.pallas import tpu as pltpu
from jax.sharding import PartitionSpec as P

MESH = pl.DeviceIdType.MESH
F32 = jnp.float32
BF16 = jnp.bfloat16
EPSILON = 1e-06
NEGATIVE = -1000000000.0
HEAD_DIM = 64
CORES = 2
LANES = 128
VMEM_LIMIT = 62 << 20
ANY = pl.BlockSpec(memory_space=pl.ANY)
VMEM = pl.BlockSpec(memory_space=pltpu.VMEM)


def nn(a, b):
    return lax.dot_general(a, b, (((1,), (0,)), ((), ())), preferred_element_type=F32)


def nt(a, b):
    return lax.dot_general(a, b, (((1,), (1,)), ((), ())), preferred_element_type=F32)


def tn(a, b):
    return lax.dot_general(a, b, (((0,), (0,)), ((), ())), preferred_element_type=F32)


class Place:
    def __init__(self, tensor, dp):
        self.tensor = tensor
        self.groups = dp // CORES
        self.chips = tensor * self.groups
        self.pipe = lax.axis_index("pipe")
        self.d = lax.axis_index("dp")
        self.t = lax.axis_index("tensor")
        self.core = lax.rem(self.d, CORES)
        self.group = self.d // CORES
        odd = lax.rem(self.group, 2)
        self.ring = self.group * tensor + self.t + odd * (tensor - 1 - 2 * self.t)

    def at(self, ring):
        group = ring // self.tensor
        along = lax.rem(ring, self.tensor)
        odd = lax.rem(group, 2)
        return group, along + odd * (self.tensor - 1 - 2 * along)

    def neighbour(self, step):
        group, t = self.at(lax.rem(self.ring + step + self.chips, self.chips))
        return {"dp": group * CORES + self.core, "tensor": t}

    def sibling(self):
        return {"dp": self.group * CORES + 1 - self.core}


def meet(devices):
    barrier = pltpu.get_barrier_semaphore()
    for device in devices:
        pl.semaphore_signal(barrier, inc=1, device_id=device, device_id_type=MESH)
    pl.semaphore_wait(barrier, len(devices))


def halves(rows, columns):
    if rows % 32 == 0:
        return [(pl.ds(k * (rows // 2), rows // 2), pl.ds(0, columns)) for k in range(2)]
    cut = columns // LANES // 2 * LANES
    return [(pl.ds(0, rows), pl.ds(0, cut)), (pl.ds(0, rows), pl.ds(cut, columns - cut))]


def gather_kernel(
    tensor, dp, rows_ref, pack_ref, length_ref, table_ref, x_ref, w_ref, lengths_ref, tables_ref,
    local_sem, block_send, block_recv, pass_send, pass_recv, small_send, small_recv,
    ring_send, ring_recv, core_send, core_recv,
):
    here = Place(tensor, dp)
    c, t, chips = here.core, here.t, here.chips
    nrow = rows_ref.shape[0]
    sibling = here.sibling()
    to_right, to_left = here.neighbour(1), here.neighbour(-1)
    others = [{"tensor": lax.rem(t + k, tensor)} for k in range(1, tensor)]
    meet([to_right, to_left, sibling] + others)

    lengths = pltpu.make_async_remote_copy(
        length_ref, lengths_ref.at[c], small_send.at[0], small_recv.at[0], device_id=sibling, device_id_type=MESH
    )
    lengths.start()
    own_lengths = pltpu.make_async_copy(length_ref, lengths_ref.at[c], local_sem.at[0])
    own_lengths.start()
    own_table = pltpu.make_async_copy(table_ref, tables_ref.at[t], local_sem.at[1])
    own_table.start()
    tables = []
    for k in range(1, tensor):
        tables.append(
            pltpu.make_async_remote_copy(
                table_ref, tables_ref.at[t], small_send.at[k], small_recv.at[k], device_id=others[k - 1], device_id_type=MESH
            )
        )
        tables[-1].start()

    def to_chip(i):
        return pltpu.make_async_remote_copy(
            rows_ref.at[i], x_ref.at[:, t], block_send.at[i], block_recv.at[t],
            device_id={"tensor": nrow * c + i}, device_id_type=MESH,
        )

    def kept(i):
        return pltpu.make_async_copy(rows_ref.at[i], x_ref.at[:, t], local_sem.at[2])

    def kept_pass(i):
        return pltpu.make_async_remote_copy(
            rows_ref.at[i], x_ref.at[:, t], pass_send.at[t], pass_recv.at[t], device_id=sibling, device_id_type=MESH
        )

    def passed(s):
        return pltpu.make_async_remote_copy(
            x_ref.at[:, s], x_ref.at[:, s], pass_send.at[s], pass_recv.at[s], device_id=sibling, device_id_type=MESH
        )

    for i in range(nrow):
        mine = nrow * c + i == t

        @pl.when(mine)
        def _():
            kept(i).start()
            kept_pass(i).start()

        @pl.when(jnp.logical_not(mine))
        def _():
            to_chip(i).start()

    parts = halves(*pack_ref.shape)
    own_pack = pltpu.make_async_copy(pack_ref, w_ref.at[t, here.d], local_sem.at[3])
    own_pack.start()

    def shard(ring, part):
        group, at = here.at(ring)
        return w_ref.at[at, group * CORES + c, parts[part][0], parts[part][1]]

    def source(step, part):
        return lax.rem(here.ring + (1 if part else -1) * step + chips, chips)

    def onward(step, part, first=False):
        slot = shard(source(step, part), part)
        return pltpu.make_async_remote_copy(
            pack_ref.at[parts[part][0], parts[part][1]] if first else slot, slot,
            ring_send.at[part, step], ring_recv.at[part, step],
            device_id=to_left if part else to_right, device_id_type=MESH,
        )

    def across(step, part, first=False):
        slot = shard(source(step, part), part)
        return pltpu.make_async_remote_copy(
            pack_ref.at[parts[part][0], parts[part][1]] if first else slot, slot,
            core_send.at[part, step], core_recv.at[part, step], device_id=sibling, device_id_type=MESH,
        )

    for part in range(2):
        onward(0, part, True).start()
        across(0, part, True).start()

    takes = t // nrow == c
    for s in range(tensor):

        @pl.when(jnp.logical_and(takes, s != t))
        def _():
            pltpu.make_async_remote_copy(
                rows_ref.at[0], x_ref.at[:, s], block_send.at[0], block_recv.at[s], device_id=sibling, device_id_type=MESH
            ).wait_recv()
            passed(s).start()

    @pl.loop(1, chips)
    def _(step):
        for part in range(2):
            onward(step - 1, part).wait_recv()

            @pl.when(step < chips - 1)
            def _():
                onward(step, part).start()

            across(step, part).start()

    @pl.loop(0, chips)
    def _(step):
        for part in range(2):

            @pl.when(step < chips - 1)
            def _():
                onward(step, part).wait_send()

            across(step, part).wait_send()
            across(step, part).wait_recv()

    for i in range(nrow):
        mine = nrow * c + i == t

        @pl.when(mine)
        def _():
            kept(i).wait()
            kept_pass(i).wait_send()

        @pl.when(jnp.logical_not(mine))
        def _():
            to_chip(i).wait_send()

    for s in range(tensor):

        @pl.when(jnp.logical_and(takes, s != t))
        def _():
            passed(s).wait_send()

        @pl.when(jnp.logical_not(takes))
        def _():
            passed(s).wait_recv()

    lengths.wait()
    own_lengths.wait()
    own_table.wait()
    own_pack.wait()
    for table in tables:
        table.wait()


def gather(tensor, dp, rows, pack, lengths, table):
    chips = tensor * dp // CORES
    nrow, two, places, width = rows.shape
    sems = pltpu.SemaphoreType.DMA
    return pl.pallas_call(
        functools.partial(gather_kernel, tensor, dp),
        out_shape=(
            jax.ShapeDtypeStruct((two, tensor, places, width), rows.dtype),
            jax.ShapeDtypeStruct((tensor, dp) + pack.shape, pack.dtype),
            jax.ShapeDtypeStruct((CORES,) + lengths.shape, lengths.dtype),
            jax.ShapeDtypeStruct((tensor,) + table.shape, table.dtype),
        ),
        in_specs=[ANY] * 4,
        out_specs=(ANY,) * 4,
        scratch_shapes=[
            sems((4,)), sems((nrow,)), sems((tensor,)), sems((tensor,)), sems((tensor,)), sems((tensor,)), sems((tensor,)),
            sems((2, chips)), sems((2, chips)), sems((2, chips)), sems((2, chips)),
        ],
        compiler_params=pltpu.CompilerParams(collective_id=0, has_side_effects=True),
        name="gather",
    )(rows, pack, lengths, table)


def scatter_kernel(
    tensor, dp, grads_ref, small_ref, rows_ref, out_ref, small_out, rows_out,
    own, theirs, taken, small_own, small_theirs, small_taken, total,
    own_sem, core_send, core_recv, ring_send, ring_recv,
    sown_sem, score_send, score_recv, sring_send, sring_recv, block_send, block_recv, local_sem,
):
    here = Place(tensor, dp)
    c, t, chips = here.core, here.t, here.chips
    nrow = rows_out.shape[0]
    sibling = here.sibling()
    to_right, to_left = here.neighbour(1), here.neighbour(-1)
    line = [
        {"dp": here.group * CORES + lax.rem(c + j, CORES), "tensor": lax.rem(t + k, tensor)}
        for j in range(CORES)
        for k in range(tensor)
        if j + k > 0
    ]
    meet([to_right, to_left] + line)

    half = tensor // 2
    owner = t // nrow

    def block(k):
        place = here.pipe * (c * half + k % half) + (1 - here.pipe) * k
        which = here.pipe * (k // half) + (1 - here.pipe) * c
        return place, which

    def home(k):
        place, which = block(k)
        slot = rows_out.at[lax.rem(t, nrow), which]
        recv = block_recv.at[lax.rem(t, nrow), which]
        return (
            jnp.logical_and(place == t, owner == c),
            lambda: pltpu.make_async_copy(rows_ref.at[k], slot, recv),
            lambda: pltpu.make_async_remote_copy(
                rows_ref.at[k], slot, block_send.at[k], recv,
                device_id={"dp": here.group * CORES + owner, "tensor": place}, device_id_type=MESH,
            ),
        )

    for k in range(tensor):
        stays, inside, away = home(k)

        @pl.when(stays)
        def _():
            inside().start()

        @pl.when(jnp.logical_not(stays))
        def _():
            away().start()

    def across(ring):
        group, at = here.at(ring)
        return (
            pltpu.make_async_remote_copy(
                grads_ref.at[at, group * CORES + 1 - c], theirs.at[ring], core_send.at[ring], core_recv.at[ring],
                device_id=sibling, device_id_type=MESH,
            ),
            pltpu.make_async_remote_copy(
                small_ref.at[at, group * CORES + 1 - c], small_theirs.at[ring], score_send.at[ring], score_recv.at[ring],
                device_id=sibling, device_id_type=MESH,
            ),
        )

    def fetch(ring):
        group, at = here.at(ring)
        return (
            pltpu.make_async_copy(grads_ref.at[at, group * CORES + c], own.at[ring], own_sem.at[ring]),
            pltpu.make_async_copy(small_ref.at[at, group * CORES + c], small_own.at[ring], sown_sem.at[ring]),
        )

    def behind(step):
        return lax.rem(here.ring - step + chips, chips)

    def order(k):
        off = (2 * lax.rem(k, 2) - 1) * (k // 2 + 1) * (1 - k // (chips - 1))
        return lax.rem(here.ring + chips + off, chips)

    @pl.loop(0, chips)
    def _(k):
        for copy in across(order(k)) + fetch(order(k)):
            copy.start()

    rows, columns = out_ref.shape
    parts = halves(rows, columns)

    def add(ring, part, step, last):
        height = parts[part][0].size
        piece = 16 if height % 16 == 0 else height

        @pl.loop(0, height // piece)
        def _(k):
            at = pl.ds(pl.multiple_of(parts[part][0].start + k * piece, 8), piece)
            where = (at, parts[part][1])
            value = own[(ring,) + where].astype(F32) + theirs[(ring,) + where].astype(F32)
            if step is not None:
                value = value + taken[(step,) + where].astype(F32)
            if last:
                total[where] = value
            else:
                own[(ring,) + where] = value.astype(BF16)

    def onward(ring, step, part):
        where = (parts[part][0], parts[part][1])
        return pltpu.make_async_remote_copy(
            own.at[(ring,) + where], taken.at[(step,) + where], ring_send.at[part, step], ring_recv.at[part, step],
            device_id=to_left if part else to_right, device_id_type=MESH,
        )

    def small_onward(ring, step):
        return pltpu.make_async_remote_copy(
            small_own.at[ring], small_taken.at[step], sring_send.at[step], sring_recv.at[step],
            device_id=to_right, device_id_type=MESH,
        )

    def ready(ring):
        for copy in across(ring):
            copy.wait_recv()
        for copy in fetch(ring):
            copy.wait()

    def ahead(step):
        return lax.rem(here.ring + step, chips)

    half_chips = chips // 2

    @pl.loop(0, chips - 1)
    def _(step):
        right, left = behind(step + 1), ahead(step + 1)

        @pl.when(step < half_chips)
        def _():
            ready(right)

        @pl.when(step < chips - 1 - half_chips)
        def _():
            ready(left)

        @pl.when(step == 0)
        def _():
            add(right, 0, None, False)
            add(left, 1, None, False)
            small_own[right] = small_own[right] + small_theirs[right]

        @pl.when(step > 0)
        def _():
            onward(right, step - 1, 0).wait_recv()
            add(right, 0, step - 1, False)
            onward(right, step, 0).start()
            onward(left, step - 1, 1).wait_recv()
            add(left, 1, step - 1, False)
            onward(left, step, 1).start()
            small_onward(right, step - 1).wait_recv()
            small_own[right] = small_own[right] + small_theirs[right] + small_taken[step - 1]
            small_onward(right, step).start()

        @pl.when(step == 0)
        def _():
            onward(right, 0, 0).start()
            onward(left, 0, 1).start()
            small_onward(right, 0).start()

    ready(here.ring)
    for part in range(2):
        onward(here.ring, chips - 2, part).wait_recv()
        add(here.ring, part, chips - 2, True)
    small_onward(here.ring, chips - 2).wait_recv()
    small_out[...] = small_own[here.ring] + small_theirs[here.ring] + small_taken[chips - 2]
    finish = pltpu.make_async_copy(total, out_ref, local_sem.at[0])
    finish.start()

    @pl.loop(0, chips)
    def _(step):
        @pl.when(step < chips - 1)
        def _():
            onward(behind(step + 1), step, 0).wait_send()
            onward(ahead(step + 1), step, 1).wait_send()
            small_onward(behind(step + 1), step).wait_send()

        for copy in across(step):
            copy.wait_send()

    for k in range(tensor):
        stays, inside, away = home(k)

        @pl.when(jnp.logical_not(stays))
        def _():
            away().wait_send()

    for i in range(nrow):
        for which in range(2):
            pltpu.make_async_copy(rows_ref.at[0], rows_out.at[i, which], block_recv.at[i, which]).wait()
    finish.wait()


def scatter(tensor, dp, grads, small, rows, nrow):
    chips = tensor * dp // CORES
    shard = grads.shape[2:]
    tiny = small.shape[2:]
    sems = pltpu.SemaphoreType.DMA
    return pl.pallas_call(
        functools.partial(scatter_kernel, tensor, dp),
        out_shape=(
            jax.ShapeDtypeStruct(shard, F32),
            jax.ShapeDtypeStruct(tiny, F32),
            jax.ShapeDtypeStruct((nrow, 2) + rows.shape[1:], rows.dtype),
        ),
        in_specs=[ANY] * 3,
        out_specs=(ANY, VMEM, ANY),
        scratch_shapes=[
            pltpu.VMEM((chips,) + shard, BF16),
            pltpu.VMEM((chips,) + shard, BF16),
            pltpu.VMEM((chips - 1,) + shard, BF16),
            pltpu.VMEM((chips,) + tiny, F32),
            pltpu.VMEM((chips,) + tiny, F32),
            pltpu.VMEM((chips - 1,) + tiny, F32),
            pltpu.VMEM(shard, F32),
            sems((chips,)), sems((chips,)), sems((chips,)), sems((2, chips)), sems((2, chips)),
            sems((chips,)), sems((chips,)), sems((chips,)), sems((chips,)), sems((chips,)),
            sems((tensor,)), sems((nrow, 2)), sems((1,)),
        ],
        compiler_params=pltpu.CompilerParams(collective_id=1, has_side_effects=True, vmem_limit_bytes=VMEM_LIMIT),
        name="scatter",
    )(grads, small, rows)


KEY, VALUE, QUERY, OUT, FIRST, SECOND = range(6)
ATTN, CROSS, INNER, OUTER = range(4)
SEGS_HELD = 6


def rms(value):
    return lax.rsqrt(jnp.mean(value * value, axis=-1, keepdims=True) + EPSILON)


def in_rows(count, body, piece=32):
    @pl.loop(0, count // piece)
    def _(k):
        body(pl.ds(pl.multiple_of(k * piece, piece), piece))


def columns_of(count, body, piece=768):
    piece = min(piece, count)

    @pl.loop(0, count // piece)
    def _(k):
        body(pl.ds(pl.multiple_of(k * piece, piece), piece))


def normalize(source, gain, target, count):
    def body(at):
        value = source[at, :].astype(F32)
        target[at, :] = (value * rms(value) * gain).astype(BF16)

    in_rows(count, body)


def normalize_back(source, gain, incoming, total, gain_parts, count, fresh):
    gain_parts[...] = jnp.zeros_like(gain_parts)

    def body(at):
        value, back = source[at, :].astype(F32), incoming[at, :]
        scale = rms(value)
        unit = value * scale
        gain_parts[...] += jnp.sum((back * unit).reshape(-1, 8, back.shape[-1]), axis=0)
        back = back * gain
        back = scale * (back - unit * jnp.mean(back * unit, axis=-1, keepdims=True))
        total[at, :] = back if fresh else total[at, :] + back

    in_rows(count, body)


def project(left, weight, target, count):
    def body(at):
        target[0:count, at] = nn(left[0:count, :], weight[:, at]).astype(target.dtype)

    columns_of(weight.shape[1], body)


def project_back(left, weight, total, count, fresh):
    def body(at):
        value = nt(left[0:count, :], weight[at, :])
        total[0:count, at] = value if fresh else total[0:count, at] + value

    columns_of(weight.shape[0], body)


def to_bf16(source, target, rows):
    def body(at):
        target[at, :] = source[at, :].astype(BF16)

    in_rows(rows, body)


def turn(left, turned, rows):
    def body(at):
        turned[at, 0:rows] = left[0:rows, at].T

    columns_of(left.shape[1], body, LANES)


def lane_half(shape, part):
    return lax.broadcasted_iota(jnp.int32, shape, 1) // HEAD_DIM == part


def attend(keys, values, queries, mixture, probs, rows, span, pairs, mask, bias, after):
    @pl.loop(0, pairs)
    def _(pair):
        lanes = pl.ds(pl.multiple_of(pair * LANES, LANES), LANES)
        key, query = keys[0:span, lanes], queries[0:rows, lanes]
        value_t = values[0:span, lanes].T
        mixed = []
        for part in range(2):
            one = jnp.where(lane_half(query.shape, part), query, jnp.zeros_like(query))
            scores = nt(key, one) + mask[0:span, 0:rows]
            if bias is not None:
                scores = scores + bias(2 * pair + part)
            scores = jnp.exp(scores - jnp.max(scores, axis=0, keepdims=True))
            scores = (scores * (1.0 / jnp.sum(scores, axis=0, keepdims=True))).astype(BF16)
            probs[2 * pair + part, 0:span, 0:rows] = scores
            mixed.append(nn(value_t[part * HEAD_DIM : (part + 1) * HEAD_DIM, :], scores))
        mixture[0:rows, lanes] = jnp.concatenate(mixed, axis=0).T.astype(BF16)
        after(pair)


def attend_back(keys, values, queries, back, probs, rows, span, pairs, each, before, after):
    @pl.loop(0, pairs)
    def _(pair):
        before(pair)
        lanes = pl.ds(pl.multiple_of(pair * LANES, LANES), LANES)
        key, value = keys[0:span, lanes], values[0:span, lanes]
        query, given = queries[0:rows, lanes], back[0:rows, lanes]
        key_t = key.T
        d_key, d_value, d_query = None, None, []
        for part in range(2):
            side = lane_half(query.shape, part)
            query_one = jnp.where(side, query, jnp.zeros_like(query))
            given_one = jnp.where(side, given, jnp.zeros_like(given))
            prob = probs[2 * pair + part, 0:span, 0:rows]
            wide = prob.astype(F32)
            d_prob = nt(value, given_one)
            d_score = (wide * (d_prob - jnp.sum(wide * d_prob, axis=0, keepdims=True))).astype(BF16)
            if each is not None:
                each(2 * pair + part, d_score)
            of_key, of_value = nn(d_score, query_one), nn(prob, given_one)
            d_key = of_key if d_key is None else d_key + of_key
            d_value = of_value if d_value is None else d_value + of_value
            d_query.append(nn(key_t[part * HEAD_DIM : (part + 1) * HEAD_DIM, :], d_score))
        keys[0:span, lanes] = d_key.astype(BF16)
        values[0:span, lanes] = d_value.astype(BF16)
        queries[0:rows, lanes] = jnp.concatenate(d_query, axis=0).T.astype(BF16)
        after(pair)


def segments(lengths_row, shape, axis, first):
    lane = lax.broadcasted_iota(jnp.int32, lengths_row.shape, 1)
    places = lax.broadcasted_iota(jnp.int32, shape, axis) + first
    ids = jnp.zeros(shape, jnp.int32)
    for c in range(SEGS_HELD):
        bound = jnp.sum(jnp.where(lane <= c, lengths_row, 0), axis=1, keepdims=True)
        ids = ids + (places >= bound).astype(jnp.int32)
    return ids


def masked(allowed):
    return jnp.where(allowed, 0.0, NEGATIVE).astype(F32)


def nothing(*unused, **named):
    pass


def work(r, here, supply, drain, tensor, heads_at):
    c, t = here.core, here.t
    width = r.hidden.shape[1]
    tall = r.hidden.shape[0]
    block = width // tensor
    half_width = width // 2
    units = r.inner.shape[2]
    places = r.x.shape[2]
    sibling = here.sibling()
    across = [{"pipe": 1 - here.pipe, "dp": here.group * CORES + k} for k in range(CORES)]
    nrow = tensor // CORES
    rows_e, span_e, rows_d, span_d = tall // 2, tall, tall // 4, tall // 2
    pairs_here = half_width // LANES
    near_lanes = pl.ds(pl.multiple_of(c * half_width, half_width), half_width)
    far_lanes = pl.ds(pl.multiple_of((1 - c) * half_width, half_width), half_width)
    lane_halves = [slice(k * half_width, (k + 1) * half_width) for k in range(CORES)]

    def move(source, target, sends, recvs, device):
        return pltpu.make_async_remote_copy(
            source, target, r.send_sem.at[sends], r.recv_sem.at[recvs], device_id=device, device_id_type=MESH
        )

    def lengths_row(first):
        return r.lengths[t // nrow, pl.ds(first + lax.rem(t, nrow), 1), :]

    def pair_lanes(pair):
        return pl.ds(pair * LANES if isinstance(pair, int) else pl.multiple_of(pair * LANES, LANES), LANES)

    def vector_row(head):
        return (head // heads_at) * 8 + lax.rem(head, heads_at)

    def bias_vectors():
        buckets = lax.broadcasted_iota(jnp.int32, r.onehot.shape, 0) == r.buckets[0:1, :]
        r.onehot[...] = buckets.astype(F32)
        for tt in range(tensor):
            r.vectors[pl.ds(8 * tt, 8), :] = lax.dot_general(
                r.tables[tt][:, 0 : r.onehot.shape[0]], r.onehot[...], (((1,), (0,)), ((), ())),
                precision=lax.Precision.HIGHEST, preferred_element_type=F32,
            )

    def rows_ready(span, rows, first_block):
        @pl.loop(0, span // places)
        def _(k):
            value = r.x[k // tensor, lax.rem(k, tensor)].astype(F32)
            at = pl.ds(pl.multiple_of(k * places, places), places)
            r.hidden[at, :] = (value * rms(value) * r.gains[0]).astype(BF16)

        for k in range(rows // places):
            r.own_x[k * places : (k + 1) * places, :] = r.x[first_block // tensor, lax.rem(first_block, tensor) + k]

    def untangle(source, first, count):
        def body(at):
            for tt in range(tensor):
                for k in range(count):
                    r.square[first + k, at, tt * block : (tt + 1) * block] = source[tt, at, k * block : (k + 1) * block]

        in_rows(width, body, 128)

    def self_forward(span, rows, first_row, group):
        def bias(head):
            pieces = []
            for j in range(span // LANES):
                start = pl.multiple_of(first_row + span - LANES - j * LANES, LANES)
                row = r.vectors[pl.ds(vector_row(head), 1), pl.ds(start, rows + LANES)]
                wide = jnp.broadcast_to(row, (LANES, rows + LANES))
                pieces.append(pltpu.roll(wide, rows + 1, 1, stride=1, stride_axis=0)[:, 0:rows])
            return jnp.concatenate(pieces, axis=0)

        untangle(r.raw_a, KEY, 2)
        untangle(r.raw_a.at[:, :, pl.ds(2 * block, 2 * block)], QUERY, 2)
        project(r.hidden, r.square.at[KEY], r.keys, span)
        supply.pump()
        project(r.hidden, r.square.at[VALUE], r.values, span)
        project(r.hidden.at[pl.ds(first_row, rows)], r.square.at[QUERY], r.queries, rows)
        supply.pump()
        after = at_each(range(width // LANES), supply.pump)

        attend(r.keys, r.values, r.queries, r.mixture, r.probs, rows, span, width // LANES, r.mask, bias, after)
        project_back(r.mixture, r.square.at[OUT], r.resid_mid, rows, True)

        def add(at):
            r.resid_mid[at, :] += r.own_x[at, :].astype(F32)

        in_rows(rows, add)
        supply.pump(until=group)
        supply.finish(group)

    def at_each(places, do):
        def hook(n):
            for place in places:

                @pl.when(n == place)
                def _():
                    do()

        return hook

    def feed_forward(rows, hook=nothing):
        @pl.loop(0, tensor)
        def _(tt):
            def body(at):
                value = nn(r.second[0:rows, :], r.inner[tt, :, at])
                cdf = 0.5 * (1.0 + lax.erf(value * 0.7071067811865476))
                r.ff[tt, 0:rows, at] = (value * cdf).astype(BF16)
                slope = cdf + value * jnp.exp(-0.5 * value * value) * 0.3989422804014327
                r.ff[tensor + tt, 0:rows, at] = slope.astype(BF16)

            columns_of(units, body)
            hook(tt)

    def feed_out(target, rows, hook=nothing):
        @pl.loop(0, tensor)
        def _(tt):
            def body(at):
                target[0:rows, at] += nt(r.ff[tt, 0:rows, :], r.outer[tt, at, :])

            columns_of(width, body)
            hook(tt)

    def feed_back(rows, ready, hook=nothing):
        r.summed[0:rows, :] = jnp.zeros((rows, width), F32)

        @pl.loop(0, tensor)
        def _(tt):
            def body(at):
                if ready:
                    value = r.ff[tensor + tt, rows : 2 * rows, at].astype(F32)
                else:
                    value = nn(r.d_branch[0:rows, :], r.outer[tt, :, at])
                r.ff[tensor + tt, 0:rows, at] = (value * r.ff[tensor + tt, 0:rows, at].astype(F32)).astype(BF16)

            columns_of(units, body)

            def back(at):
                r.summed[0:rows, at] += nt(r.ff[tensor + tt, 0:rows, :], r.inner[tt, at, :])

            columns_of(width, back)
            hook(tt)

    def feed_grads(rows, turned, first, which, hook=nothing):
        @pl.loop(0, tensor)
        def _(tt):
            slot = lax.rem(tt, 2)

            @pl.when(tt >= 2)
            def _():
                drain.release(which, tt - 2, slot)

            def body(at):
                r.stage[slot, :, at] = nn(turned[:, 0:rows], r.ff[first + tt, 0:rows, at]).astype(BF16)

            columns_of(units, body)
            drain.emit(which, tt, slot)
            hook(tt)

        for tt in range(tensor - 2, tensor):
            drain.release(which, tt, tt % 2)

    def square_grads(rows, which, products, hook):
        for k in range(tensor // 2):
            for j, (turned, right) in enumerate(products):

                def body(at):
                    value = nn(turned[at, 0:rows], right[0:rows, 2 * k * block : 2 * (k + 1) * block]).astype(BF16)
                    for slot in range(2):
                        r.stage[slot, at, j * block : (j + 1) * block] = value[:, slot * block : (slot + 1) * block]

                in_rows(width, body, 256)
            for slot in range(2):
                drain.emit(which, 2 * k + slot, slot)
            hook(k)
            for slot in range(2):
                drain.release(which, 2 * k + slot, slot)

    def gain_done(which):
        r.gains_out[which : which + 1, :] = jnp.sum(r.gain_parts[...], axis=0, keepdims=True)

    def self_backward(span, rows, first_row, steps, send_rows):
        mirror = (
            lax.broadcasted_iota(jnp.int32, (LANES, LANES), 0) + lax.broadcasted_iota(jnp.int32, (LANES, LANES), 1)
            == LANES - 1
        ).astype(BF16)
        to_bf16(r.d_resid, r.branch, rows)
        project(r.branch, r.square.at[OUT], r.d_branch, rows)
        r.diagonals[...] = jnp.zeros_like(r.diagonals)

        def each(head, d_score):
            for j in range(span // LANES):
                start = pl.multiple_of(first_row + span - LANES - j * LANES, LANES)
                piece = nn(mirror, d_score[j * LANES : (j + 1) * LANES, :])
                piece = jnp.concatenate([piece, jnp.zeros((LANES, LANES), F32)], axis=1)
                piece = pltpu.roll(piece, 0, 1, stride=1, stride_axis=0)
                at = (pl.ds(vector_row(head), 1), pl.ds(start, rows + LANES))
                r.diagonals[at] += jnp.sum(piece, axis=0, keepdims=True)

        pairs = width // LANES
        attend_back(
            r.keys, r.values, r.queries, r.d_branch, r.probs, rows, span, pairs, each, nothing,
            at_each(range(pairs), steps),
        )
        far = pl.ds(pl.multiple_of((1 - c) * rows, rows), rows)
        near = pl.ds(pl.multiple_of(c * rows, rows), rows)
        trades = [
            move(source.at[far], r.taken_pair.at[k, pl.ds(0, rows)], 12 + k, 12 + k, sibling)
            for k, source in enumerate((r.keys, r.values))
        ]
        for trade in trades:
            trade.start()
        steps()
        turn(r.branch, r.turned, rows)
        turn(r.hidden.at[pl.ds(first_row, rows)], r.turned_more, rows)
        for tt in range(tensor):
            at = pl.ds(8 * tt, 8)
            r.bias_out[at, 0 : r.onehot.shape[0]] = lax.dot_general(
                r.diagonals[at, :], r.onehot[...], (((1,), (1,)), ((), ())),
                precision=lax.Precision.HIGHEST, preferred_element_type=F32,
            )
        steps()
        project_back(r.queries, r.square.at[QUERY], r.summed, rows, True)
        for trade in trades:
            trade.wait_recv()
        steps()
        for k, source in enumerate((r.keys, r.values)):
            r.d_pair[k, 0:rows, :] = (source[near, :].astype(F32) + r.taken_pair[k, 0:rows, :].astype(F32)).astype(BF16)
        project_back(r.d_pair.at[0], r.square.at[KEY], r.summed, rows, False)
        project_back(r.d_pair.at[1], r.square.at[VALUE], r.summed, rows, False)
        steps()
        normalize_back(r.own_x, r.gains[0], r.summed, r.d_resid, r.gain_parts, rows, False)
        gain_done(0)
        steps()
        send_rows()
        drain.small_begin()
        drain.allow(2)
        products = [(r.turned_more, r.d_pair.at[0]), (r.turned_more, r.d_pair.at[1]), (r.turned_more, r.queries), (r.turned, r.mixture)]
        square_grads(rows, ATTN, products, nothing)
        for trade in trades:
            trade.wait_send()
        steps()
        drain.begin(ATTN)
        steps()
        drain.rest(ATTN)

    def parts_of(array):
        return [array.at[pl.ds(k * rows_d, rows_d)] for k in range(CORES)]

    def part_here(array):
        return array.at[pl.ds(pl.multiple_of(c * rows_d, rows_d), rows_d)]

    r.gains_out[...] = jnp.zeros_like(r.gains_out)
    r.bias_out[...] = jnp.zeros_like(r.bias_out)
    supply.start()

    def entry():
        supply.pump(2)
        supply.small()
        bias_vectors()
        supply.pump(2)
        supply.rows()

    def schedule(*items):
        left = list(items)

        def steps():
            for name, group, *n in left.pop(0) if left else ():
                getattr(drain, name)(group, *n)

        return steps

    @pl.when(here.pipe == 0)
    def _():
        supply.resume(ATTN, INNER, OUTER, CROSS)
        drain.order(CROSS, OUTER, INNER, ATTN)
        entry()
        rows, span = rows_e, span_e
        first_row = pl.multiple_of(c * rows, rows)
        seg_rows = segments(lengths_row(0), (span, 1), 0, 0)
        r.mask[...] = masked(seg_rows == segments(lengths_row(0), (1, rows), 1, first_row))
        supply.pump()
        rows_ready(span, rows, c * tensor)
        supply.pump(until=ATTN)
        supply.finish(ATTN)
        self_forward(span, rows, first_row, INNER)
        normalize(r.resid_mid, r.gains[1], r.second, rows)
        feed_forward(rows, at_each((1, 2, 3), supply.pump))
        supply.pump(until=OUTER)
        supply.finish(OUTER)
        r.resid_top[...] = r.resid_mid[...]
        feed_out(r.resid_top, rows, at_each((1, 2, 3), supply.pump))
        normalize(r.resid_top, r.gains[2], r.third, rows)
        r.mask[...] = masked(seg_rows == segments(lengths_row(nrow), (1, span_d), 1, 0))
        supply.pump(until=CROSS)
        supply.finish(CROSS)
        untangle(r.raw_c, FIRST, 2)
        mine = pl.ds(first_row, rows)
        other = pl.ds(pl.multiple_of((1 - c) * rows, rows), rows)
        trades = []
        for k, held in enumerate((r.cross_keys, r.cross_values)):
            r.send_pair[k] = nn(r.third[...], r.square[FIRST + k, :, far_lanes]).astype(BF16)
            trades.append(move(r.send_pair.at[k], held.at[mine], k, k, sibling))
            trades[-1].start()
        for k, held in enumerate((r.cross_keys, r.cross_values)):
            held[mine, :] = nn(r.third[...], r.square[FIRST + k, :, near_lanes]).astype(BF16)
        for k, part in enumerate(parts_of(r.cross_queries)):
            move(part, part, 2 + k, 2 + k, across[k]).wait_recv()
        for k, held in enumerate((r.cross_keys, r.cross_values)):
            move(r.send_pair.at[k], held.at[other], k, k, sibling).wait_recv()

        def mixtures(pair):
            at = pair_lanes(pair)
            return [
                pltpu.make_async_remote_copy(
                    r.cross_mixture.at[pl.ds(k * rows_d, rows_d), at], r.cross_in.at[c, :, at],
                    r.mix_send.at[k, pair], r.mix_recv.at[c, pair], device_id=across[k], device_id_type=MESH,
                )
                for k in range(CORES)
            ]

        def arrived(pair):
            for k in range(CORES):
                part = r.cross_back.at[pl.ds(k * rows_d, rows_d), pair_lanes(pair)]
                pltpu.make_async_remote_copy(
                    part, part, r.back_send.at[k, pair], r.back_recv.at[k, pair], device_id=across[k], device_id_type=MESH
                ).wait_recv()

        def returns(pair):
            at = pair_lanes(pair)
            return [
                pltpu.make_async_remote_copy(
                    d_cross.at[other, at], r.cross_taken.at[k, :, at],
                    r.give_send.at[k, pair], r.give_recv.at[k, pair], device_id=sibling, device_id_type=MESH,
                )
                for k, d_cross in enumerate((r.cross_keys, r.cross_values))
            ]

        attend(
            r.cross_keys, r.cross_values, r.cross_queries, r.cross_mixture, r.cross_probs, span_d, span, pairs_here,
            r.mask, None, lambda pair: [mix.start() for mix in mixtures(pair)],
        )
        supply.close()
        drain.free(0)
        turn(r.third, r.turned, rows)
        attend_back(
            r.cross_keys, r.cross_values, r.cross_queries, r.cross_back, r.cross_probs, span_d, span, pairs_here, None,
            arrived, lambda pair: [back.start() for back in returns(pair)],
        )
        answers = [
            move(part, r.cross_in_back.at[c], 8 + k, 8 + c, across[k]) for k, part in enumerate(parts_of(r.cross_queries))
        ]
        for answer in answers:
            answer.start()
        for k, d_cross in enumerate((r.cross_keys, r.cross_values)):
            r.d_pair[k, :, near_lanes] = d_cross[mine, :]
        for pair in range(pairs_here):
            for back in returns(pair):
                back.wait_recv()
        for k in range(2):
            r.d_pair[k, :, far_lanes] = r.cross_taken[k]
        drain.allow(0)
        square_grads(rows, CROSS, [(r.turned, r.d_pair.at[0]), (r.turned, r.d_pair.at[1])], nothing)
        drain.begin(CROSS)
        project_back(r.d_pair.at[0], r.square.at[FIRST], r.summed, rows, True)
        project_back(r.d_pair.at[1], r.square.at[SECOND], r.summed, rows, False)
        normalize_back(r.resid_top, r.gains[2], r.summed, r.d_resid, r.gain_parts, rows, True)
        gain_done(2)
        to_bf16(r.d_resid, r.d_branch, rows)
        turn(r.d_branch, r.turned, rows)
        feed_grads(rows, r.turned, 0, OUTER, at_each((2,), lambda: drain.tick(CROSS, 0)))
        drain.tick(CROSS, 1)
        drain.begin(OUTER)
        feed_back(rows, False, at_each((1, 2), schedule([("tick", CROSS, 2)], [("tick", CROSS, 3)])))
        drain.free(1)
        drain.free(2)
        turn(r.second, r.turned, rows)
        drain.allow(1)
        feed_grads(rows, r.turned, tensor, INNER, at_each((1,), lambda: drain.tick(OUTER, 0)))
        normalize_back(r.resid_mid, r.gains[1], r.summed, r.d_resid, r.gain_parts, rows, False)
        gain_done(1)
        for copy in trades + answers:
            copy.wait_send()
        for pair in range(pairs_here):
            for copy in mixtures(pair) + returns(pair):
                copy.wait_send()

        def send_rows():
            to_bf16(r.d_resid, r.rows_out, rows)
            drain.home()

        steps = schedule(
            [("tick", CROSS, 4), ("begin", INNER), ("tick", OUTER, 1)], [("end", CROSS), ("tick", OUTER, 2)],
            [], [("tick", INNER, 0)], [], [],
            [], [], [("tick", INNER, 1)], [], [("tick", OUTER, 3), ("tick", OUTER, 4)], [],
            [("tick", INNER, 2), ("tick", ATTN, 0), ("end", OUTER), ("tick", INNER, 3), ("tick", ATTN, 1), ("tick", ATTN, 2)]
            + [("home_done", None), ("tick", INNER, 4), ("tick", ATTN, 3), ("tick", ATTN, 4), ("end", INNER)],
        )
        self_backward(span, rows, first_row, steps, send_rows)

    @pl.when(here.pipe == 1)
    def _():
        supply.resume(ATTN, CROSS, INNER, OUTER)
        drain.order(OUTER, INNER, CROSS, ATTN)
        entry()
        rows, span = rows_d, span_d
        first_row = pl.multiple_of(c * rows, rows)
        key_at = lax.broadcasted_iota(jnp.int32, (span, rows), 0)
        query_at = lax.broadcasted_iota(jnp.int32, (span, rows), 1) + first_row
        same = segments(lengths_row(nrow), (span, 1), 0, 0) == segments(lengths_row(nrow), (1, rows), 1, first_row)
        r.mask[0:span, 0:rows] = masked(same & (query_at >= key_at))
        supply.pump()
        first_block = c * (tensor // 2)
        rows_ready(span, rows, first_block)
        for k in range(rows // places):
            r.d_branch[k * places : (k + 1) * places, :] = r.x[1, first_block + k]
        supply.pump(until=ATTN)
        supply.finish(ATTN)
        self_forward(span, rows, first_row, CROSS)
        untangle(r.raw_c, FIRST, 2)
        normalize(r.resid_mid, r.gains[1], r.third, rows)
        project(r.third, r.square.at[FIRST], r.joined, rows)
        asks = []
        for k in range(CORES):
            r.send_pair[k, 0:rows, :] = r.joined[:, lane_halves[k]]
            asks.append(move(r.send_pair.at[k, pl.ds(0, rows)], part_here(r.cross_queries), 2 + k, 2 + c, across[k]))
            asks[-1].start()
        supply.pump(until=INNER)
        supply.finish(INNER)
        supply.pump(until=OUTER)
        supply.finish(OUTER)

        @pl.loop(0, tensor)
        def _(tt):
            def body(at):
                r.ff[tensor + tt, rows : 2 * rows, at] = nn(r.d_branch[0:rows, :], r.outer[tt, :, at]).astype(BF16)

            columns_of(units, body)

        supply.close()
        drain.free(0)
        r.resid_top[0:rows, :] = r.resid_mid[0:rows, :]
        for k in range(CORES):
            for pair in range(pairs_here):
                part = r.cross_in.at[k, :, pair_lanes(pair)]
                pltpu.make_async_remote_copy(
                    part, part, r.mix_send.at[k, pair], r.mix_recv.at[k, pair], device_id=across[k], device_id_type=MESH
                ).wait_recv()
            r.joined[:, lane_halves[k]] = r.cross_in[k]
        project_back(r.joined, r.square.at[SECOND], r.resid_top, rows, False)
        normalize(r.resid_top, r.gains[2], r.second, rows)
        feed_forward(rows)
        feed_back(rows, True)
        r.d_resid[0:rows, :] = r.d_branch[0:rows, :].astype(F32)
        normalize_back(r.resid_top, r.gains[2], r.summed, r.d_resid, r.gain_parts, rows, False)
        gain_done(2)
        to_bf16(r.d_resid, r.branch, rows)
        tells = []
        for pair in range(pairs_here):
            for k in range(CORES):
                at = pair_lanes(pair)
                first = k * half_width + pair * LANES
                r.send_back[k, :, at] = nn(r.branch[0:rows, :], r.square[SECOND, :, first : first + LANES]).astype(BF16)
                tells.append(
                    pltpu.make_async_remote_copy(
                        r.send_back.at[k, :, at], r.cross_back.at[pl.ds(pl.multiple_of(c * rows, rows), rows), at],
                        r.back_send.at[k, pair], r.back_recv.at[c, pair], device_id=across[k], device_id_type=MESH,
                    )
                )
                tells[-1].start()
        drain.free(1)
        turn(r.d_branch, r.turned, rows)
        drain.allow(0)
        feed_grads(rows, r.turned, 0, OUTER)
        drain.begin(OUTER)
        turn(r.second, r.turned, rows)
        drain.allow(1)
        feed_grads(rows, r.turned, tensor, INNER)
        drain.begin(INNER)
        feed_out(r.resid_top, rows, at_each((1,), lambda: drain.tick(OUTER, 0)))
        drain.free(2)
        to_bf16(r.resid_top, r.rows_out, rows)
        turn(r.branch, r.turned, rows)
        turn(r.third, r.turned_more, rows)
        for k in range(CORES):
            move(r.cross_in_back.at[k], r.cross_in_back.at[k], 8 + k, 8 + k, across[k]).wait_recv()
            r.d_pair[1, 0:rows, lane_halves[k]] = r.cross_in_back[k]
        project_back(r.d_pair.at[1], r.square.at[FIRST], r.summed, rows, True)
        square_grads(rows, CROSS, [(r.turned_more, r.d_pair.at[1]), (r.turned, r.joined)], nothing)
        drain.tick(OUTER, 1)
        normalize_back(r.resid_mid, r.gains[1], r.summed, r.d_resid, r.gain_parts, rows, False)
        gain_done(1)
        for copy in asks + tells:
            copy.wait_send()

        def send_rows():
            to_bf16(r.d_resid, r.rows_out.at[pl.ds(rows, rows)], rows)
            drain.home()

        steps = schedule(
            [], [("tick", INNER, 0)], [], [("tick", INNER, 1)], [("tick", OUTER, 2)], [],
            [("tick", OUTER, 3)], [], [("tick", INNER, 2), ("tick", OUTER, 4)], [("begin", CROSS)],
            [("tick", INNER, 3), ("tick", INNER, 4)], [],
            [("end", OUTER), ("tick", CROSS, 0), ("tick", ATTN, 0), ("tick", CROSS, 1), ("end", INNER), ("tick", ATTN, 1)]
            + [("tick", ATTN, 2), ("tick", CROSS, 2), ("home_done", None), ("tick", ATTN, 3), ("tick", ATTN, 4)]
            + [("tick", CROSS, 3), ("tick", CROSS, 4), ("end", CROSS)],
        )
        self_backward(span, rows, first_row, steps, send_rows)

    drain.close()


def held(*shape, dtype=BF16):
    return pltpu.VMEM(shape, dtype)


def arrays(tensor, heads_at, places, width, units, ranges, kinds):
    tall = 2 * tensor * places
    block = width // tensor
    half_rows, half_width = tall // 2, width // 2
    heads = heads_at * tensor
    return dict(
        x=held(2, tensor, places, width),
        own_x=held(half_rows, width),
        raw_a=held(tensor, width, 4 * block),
        raw_c=held(tensor, width, 2 * block),
        square=held(6, width, width),
        inner=held(tensor, width, units),
        outer=held(tensor, width, units),
        hidden=held(tall, width),
        keys=held(tall, width),
        values=held(tall, width),
        queries=held(half_rows, width),
        probs=held(heads, tall, half_rows),
        mask=held(tall, half_rows, dtype=F32),
        mixture=held(half_rows, width),
        resid_mid=held(half_rows, width, dtype=F32),
        resid_top=held(half_rows, width, dtype=F32),
        d_resid=held(half_rows, width, dtype=F32),
        summed=held(half_rows, width, dtype=F32),
        second=held(half_rows, width),
        third=held(half_rows, width),
        ff=held(2 * tensor, half_rows, units),
        d_branch=held(half_rows, width),
        branch=held(half_rows, width),
        cross_keys=held(tall, half_width),
        cross_values=held(tall, half_width),
        cross_queries=held(half_rows, half_width),
        cross_mixture=held(half_rows, half_width),
        cross_probs=held(heads // CORES, tall, half_rows),
        cross_back=held(half_rows, half_width),
        cross_in=held(CORES, half_rows // 2, half_width),
        cross_in_back=held(CORES, half_rows // 2, half_width),
        cross_taken=held(CORES, half_rows, half_width),
        send_pair=held(CORES, half_rows, half_width),
        send_back=held(CORES, half_rows // 2, half_width),
        joined=held(half_rows // 2, width),
        taken_pair=held(2, half_rows, width),
        d_pair=held(2, half_rows, width),
        turned=held(width, half_rows),
        turned_more=held(width, half_rows),
        stage=held(2, width, units),
        vectors=held(8 * tensor, ranges, dtype=F32),
        diagonals=held(8 * tensor, ranges, dtype=F32),
        onehot=held(kinds, ranges, dtype=F32),
        gain_parts=held(8, width, dtype=F32),
        send_sem=pltpu.SemaphoreType.DMA((14,)),
        recv_sem=pltpu.SemaphoreType.DMA((14,)),
        **{
            name: pltpu.SemaphoreType.DMA((CORES, half_width // LANES))
            for name in ("mix_send", "mix_recv", "back_send", "back_recv", "give_send", "give_recv")
        },
    )


def group_columns(block, units):
    return {ATTN: (0, 4 * block), CROSS: (4 * block, 2 * block), INNER: (6 * block, units), OUTER: (6 * block + units, units)}


def landing(r):
    return {ATTN: r.raw_a, CROSS: r.raw_c, INNER: r.inner, OUTER: r.outer}


class Loads:
    def __init__(self, r, tensor, x_hbm, w_hbm, sems):
        columns = group_columns(r.raw_a.shape[2] // 4, r.inner.shape[2])
        self.x = pltpu.make_async_copy(x_hbm, r.x, sems.at[4, 0])
        self.weights = [
            [
                pltpu.make_async_copy(w_hbm.at[tt, :, pl.ds(*columns[group])], target.at[tt], sems.at[group, tt])
                for tt in range(tensor)
            ]
            for group, target in landing(r).items()
        ]

    def start(self):
        self.x.start()
        for group in self.weights:
            for copy in group:
                copy.start()

    def rows(self):
        self.x.wait()

    def finish(self, group):
        for copy in self.weights[group]:
            copy.wait()

    small = resume = pump = close = nothing


class Stores:
    def __init__(self, r, grads_hbm, sems):
        self.columns = group_columns(r.raw_a.shape[2] // 4, r.inner.shape[2])
        self.r, self.grads, self.sems = r, grads_hbm, sems

    def copy(self, group, tt, slot):
        first, wide = self.columns[group]
        return pltpu.make_async_copy(
            self.r.stage.at[slot, :, pl.ds(0, wide)], self.grads.at[tt, :, pl.ds(first, wide)], self.sems.at[slot]
        )

    def emit(self, group, tt, slot):
        self.copy(group, tt, slot).start()

    def release(self, group, tt, slot):
        self.copy(group, tt, slot).wait()

    order = free = allow = begin = tick = rest = end = home = home_done = small_begin = close = nothing


def blocks_kernel(tensor, dp, heads_at, names, *refs):
    here = Place(tensor, dp)
    r = types.SimpleNamespace(**dict(zip(names, refs)))
    across = [{"pipe": 1 - here.pipe, "dp": here.group * CORES + k} for k in range(CORES)]
    meet([here.sibling()] + across)
    work(r, here, Loads(r, tensor, r.x_hbm, r.w_hbm, r.load_sem), Stores(r, r.grads_hbm, r.stage_sem), tensor, heads_at)


def blocks(tensor, dp, heads_at, kinds, rows, weights, gains, lengths, tables, buckets):
    places, width = rows.shape[2:]
    units = (weights.shape[2] - 6 * (width // tensor)) // 2
    half_rows = tensor * places
    scratch = arrays(tensor, heads_at, places, width, units, buckets.shape[1], kinds)
    scratch["load_sem"] = pltpu.SemaphoreType.DMA((5, tensor))
    scratch["stage_sem"] = pltpu.SemaphoreType.DMA((2,))
    names = ["x_hbm", "w_hbm", "gains", "lengths", "tables", "buckets", "grads_hbm", "rows_out", "gains_out", "bias_out"]
    return pl.pallas_call(
        functools.partial(blocks_kernel, tensor, dp, heads_at, names + list(scratch)),
        out_shape=(
            jax.ShapeDtypeStruct(weights.shape, BF16),
            jax.ShapeDtypeStruct((half_rows, width), BF16),
            jax.ShapeDtypeStruct((8, width), F32),
            jax.ShapeDtypeStruct((8 * tensor, LANES), F32),
        ),
        in_specs=[ANY, ANY] + [VMEM] * 4,
        out_specs=(ANY, VMEM, VMEM, VMEM),
        scratch_shapes=list(scratch.values()),
        compiler_params=pltpu.CompilerParams(collective_id=2, has_side_effects=True, vmem_limit_bytes=VMEM_LIMIT),
        name="blocks",
    )(rows, weights, gains, lengths, tables, buckets)


class Rings:
    def __init__(self, r, here, tensor, dp):
        self.r, self.here, self.tensor, self.dp = r, here, tensor, dp
        self.depth = r.value_w.shape[0]
        self.hops = here.chips // 2
        self.count = 2 * self.hops - 1
        self.sibling = here.sibling()
        self.targets = [here.neighbour(1), here.neighbour(-1)]
        self.landing = landing(r)
        self.groups = []
        self.plan = []


    def order(self, *groups):
        steps = []
        for k, group in enumerate(groups):
            steps.append((4 * k - 0.5, k, self.begin, group, None))
            late = {self.count - 3: 3.6, self.count - 2: 3.7, self.count - 1: 5.5}
            steps += [(4 * k + late.get(n, n), k, self.tick, group, n) for n in range(self.count)]
        steps.sort(key=lambda step: step[:2])
        self.groups = list(groups)
        self.plan = [step[2:] for step in steps]

    def resume(self, *groups):
        self.order(*groups)
        self.plan.pop(0)

    def pump(self, count=1, until=None):
        while self.plan and (count > 0 if until is None else any(step[1] == until for step in self.plan)):
            do, group, n = self.plan.pop(0)
            do(group) if n is None else do(group, n)
            count -= 0 if n is None else 1


    def block_out(self, i):
        r, t, c = self.r, self.here.t, self.here.core
        return pltpu.make_async_remote_copy(
            r.rows.at[i], r.x.at[:, t], r.block_send.at[i], r.block_recv.at[t],
            device_id={"tensor": r.rows.shape[0] * c + i}, device_id_type=MESH,
        )

    def block_kept(self, i):
        return pltpu.make_async_copy(self.r.rows.at[i], self.r.x.at[:, self.here.t], self.r.local_sem.at[0])

    def block_pass(self, source, s):
        r = self.r
        return pltpu.make_async_remote_copy(
            source, r.x.at[:, s], r.pass_send.at[s], r.pass_recv.at[s], device_id=self.sibling, device_id_type=MESH
        )

    def blocks(self, mine, others):
        for i in range(self.r.rows.shape[0]):
            here = self.r.rows.shape[0] * self.here.core + i == self.here.t

            @pl.when(here)
            def _():
                mine(i)

            @pl.when(jnp.logical_not(here))
            def _():
                others(i)

    def small_copies(self):
        r, t = self.r, self.here.t
        copies = [
            pltpu.make_async_remote_copy(
                r.lengths_in, r.lengths.at[self.here.core], r.small_send.at[0], r.small_recv.at[0],
                device_id=self.sibling, device_id_type=MESH,
            ),
            pltpu.make_async_copy(r.lengths_in, r.lengths.at[self.here.core], r.local_sem.at[1]),
            pltpu.make_async_copy(r.table_in, r.tables.at[t], r.local_sem.at[2]),
        ]
        for k in range(1, self.tensor):
            copies.append(
                pltpu.make_async_remote_copy(
                    r.table_in, r.tables.at[t], r.small_send.at[k], r.small_recv.at[k],
                    device_id={"tensor": lax.rem(t + k, self.tensor)}, device_id_type=MESH,
                )
            )
        return copies


    def rows_of(self, ring):
        line, at = self.here.at(ring)
        return at, pl.multiple_of((line * CORES + self.here.core) * self.depth, 16)

    def ring_at(self, step, part):
        way = -1 if part else 1
        return lax.rem(self.here.ring - way * step + self.here.chips, self.here.chips)

    def onward(self, group, step, part, sub):
        r, half = self.r, self.depth // 2
        at, first = self.rows_of(self.ring_at(step, part))
        target = self.landing[group]
        slot = target.at[at, pl.ds(pl.multiple_of(first + half * sub, 16), half), :]
        packed = r.stage.at[0, pl.ds(group * self.depth + half * sub, half), pl.ds(0, target.shape[2])]
        return pltpu.make_async_remote_copy(
            packed if step == 0 else slot, slot, r.ring_send.at[group, part, sub, step], r.ring_recv.at[group, part, sub, step],
            device_id=self.targets[part], device_id_type=MESH,
        )

    def over(self, group, ring, first_time=False):
        r = self.r
        at, first = self.rows_of(ring)
        target = self.landing[group]
        slot = target.at[at, pl.ds(first, self.depth), :]
        packed = r.stage.at[0, pl.ds(group * self.depth, self.depth), pl.ds(0, target.shape[2])]
        return pltpu.make_async_remote_copy(
            packed if first_time else slot, slot, r.over_send.at[group, ring], r.over_recv.at[group, ring],
            device_id=self.sibling, device_id_type=MESH,
        )

    def own(self, group):
        wide = self.landing[group].shape[2]
        first = pl.multiple_of(self.here.d * self.depth, 16)
        return pltpu.make_async_copy(
            self.r.stage.at[0, pl.ds(group * self.depth, self.depth), pl.ds(0, wide)],
            self.landing[group].at[self.here.t, pl.ds(first, self.depth), :],
            self.r.own_sem.at[group],
        )

    def begin(self, group):
        for sub in range(2):
            for part in range(2):
                self.onward(group, 0, part, sub).start()
        self.over(group, self.here.ring, True).start()
        self.own(group).start()

    def tick(self, group, n):
        step, last = n // 2 + 1, n == self.count - 1
        for part in range(2):
            sub = part if last else n % 2
            self.onward(group, step - 1, part, sub).wait_recv()
            if not last and (step < self.hops - 1 or sub == part):
                self.onward(group, step, part, sub).start()
        if last:
            self.over(group, self.ring_at(step, 0)).start()
        elif n % 2:
            for part in range(2):
                self.over(group, self.ring_at(step, part)).start()

    def sends_done(self, group):
        for part in range(2):
            for sub in range(2):
                for step in range(self.hops):
                    if step < self.hops - 1 or sub == part:
                        self.onward(group, step, part, sub).wait_send()

    def finish(self, group):
        @pl.loop(0, self.here.chips)
        def _(ring):
            self.over(group, ring).wait_recv()

        self.own(group).wait()

    def start(self):
        r, depth = self.r, self.depth
        nrow = r.rows.shape[0]
        r.lengths_in[...] = jnp.zeros_like(r.lengths_in)
        r.lengths_in[0:nrow, 0 : r.enc_lengths.shape[1]] = r.enc_lengths[...]
        r.lengths_in[nrow : 2 * nrow, 0 : r.dec_lengths.shape[1]] = r.dec_lengths[...]
        r.table_in[...] = jnp.zeros_like(r.table_in)
        for k in range(r.bias_w.shape[0]):
            r.table_in[k : k + 1, 0 : r.bias_w.shape[2]] = r.bias_w[k]
        self.blocks(
            lambda i: (self.block_kept(i).start(), self.block_pass(r.rows.at[i], self.here.t).start()),
            lambda i: self.block_out(i).start(),
        )
        block = r.value_w.shape[1]

        def band(group, pieces):
            wide = pieces[0].shape[1]
            for k, piece in enumerate(pieces):
                r.stage[0, group * depth : (group + 1) * depth, k * wide : (k + 1) * wide] = piece

        band(ATTN, [r.query_key_w[1], r.value_w[...], r.query_key_w[0], r.out_w[...].T])
        self.order(ATTN)
        self.begin(ATTN)
        for copy in self.small_copies():
            copy.start()
        band(INNER, [r.inner_w[...]])
        band(OUTER, [r.outer_w[...]])
        band(CROSS, [r.first_w[...], r.second_w[...]])

    def small(self):
        for copy in self.small_copies():
            copy.wait()

    def rows(self):
        r, t = self.r, self.here.t
        takes = lax.div(t, r.rows.shape[0]) == self.here.core
        for s in range(self.tensor):

            @pl.when(jnp.logical_and(takes, s != t))
            def _():
                pltpu.make_async_remote_copy(
                    r.rows.at[0], r.x.at[:, s], r.block_send.at[0], r.block_recv.at[s],
                    device_id=self.sibling, device_id_type=MESH,
                ).wait_recv()
                self.block_pass(r.x.at[:, s], s).start()

        self.blocks(lambda i: self.block_kept(i).wait(), nothing)
        for s in range(self.tensor):

            @pl.when(jnp.logical_not(takes))
            def _():
                self.block_pass(r.x.at[:, s], s).wait_recv()

    def close(self):
        r, t = self.r, self.here.t
        takes = lax.div(t, r.rows.shape[0]) == self.here.core
        self.blocks(
            lambda i: self.block_pass(r.rows.at[i], t).wait_send(),
            lambda i: self.block_out(i).wait_send(),
        )
        for s in range(self.tensor):

            @pl.when(jnp.logical_and(takes, s != t))
            def _():
                self.block_pass(r.x.at[:, s], s).wait_send()

        for group in self.groups:
            self.sends_done(group)

            @pl.loop(0, self.here.chips)
            def _(ring):
                self.over(group, ring).wait_send()


class Sums:
    def __init__(self, r, here, tensor, dp):
        self.r, self.here, self.tensor, self.dp = r, here, tensor, dp
        self.depth = r.value_w.shape[0]
        self.hops = here.chips // 2
        self.count = 2 * self.hops - 3
        self.sibling = here.sibling()
        self.targets = [here.neighbour(1), here.neighbour(-1)]
        self.box = {CROSS: r.raw_c, OUTER: r.raw_a, INNER: r.inner, ATTN: r.outer}
        self.kept = {CROSS: r.own_cross, OUTER: r.own_outer, INNER: r.own_inner, ATTN: r.ff}
        self.groups = []

    def order(self, *groups):
        self.groups = list(groups)

    def free(self, k):
        for device in self.targets + [self.sibling]:
            pl.semaphore_signal(self.r.free_sem.at[k], inc=1, device_id=device, device_id_type=MESH)

    def allow(self, k):
        pl.semaphore_wait(self.r.free_sem.at[k], 3)

    def boxed(self, group, index, first, height):
        if isinstance(index, int):
            return (index // self.dp, pl.ds(pl.multiple_of(index % self.dp * self.depth + first, 16), height), slice(None))
        at = pl.ds(pl.multiple_of(lax.rem(index, self.dp) * self.depth + first, 16), height)
        return (lax.div(index, self.dp), at, slice(None))

    def taken(self, group, step, part, first, height):
        index = step + part * (self.hops - 1) if step else 0
        return self.boxed(group, index, first, height)

    def theirs(self, group, ring, first, height):
        return self.boxed(group, self.here.chips - 1 + ring, first, height)

    def own(self, group, ring, first, height):
        return (ring, pl.ds(first, height), slice(None))

    def ring_of(self, line, at):
        return line * self.tensor + at + (line % 2) * (self.tensor - 1 - 2 * at)

    def pieces(self, group, tt, slot):
        r, depth = self.r, self.depth
        wide = self.box[group].shape[2]
        made = []
        for line in range(self.here.groups):
            ring = self.ring_of(line, tt)

            def rows_of(core):
                return r.stage.at[slot, pl.ds(pl.multiple_of((line * CORES + core) * depth, 16), depth), pl.ds(0, wide)]

            made.append(
                pltpu.make_async_copy(
                    rows_of(self.here.core), self.kept[group].at[self.own(group, ring, 0, depth)], r.kept_sem.at[slot, line]
                )
            )
            made.append(
                pltpu.make_async_remote_copy(
                    rows_of(1 - self.here.core), self.box[group].at[self.theirs(group, ring, 0, depth)],
                    r.over_send.at[group, ring], r.over_recv.at[group, ring], device_id=self.sibling, device_id_type=MESH,
                )
            )
        return made

    def emit(self, group, tt, slot):
        for piece in self.pieces(group, tt, slot):
            piece.start()

    def release(self, group, tt, slot):
        for k, piece in enumerate(self.pieces(group, tt, slot)):
            if k % 2:
                piece.wait_send()
            else:
                piece.wait()


    def rows_at(self, sub):
        half = self.depth // 2
        return half * sub, half

    def source(self, step, part):
        way = -1 if part else 1
        return lax.rem(self.here.ring + way * (self.hops - step) + self.here.chips, self.here.chips)

    def onward(self, group, step, part, sub):
        r = self.r
        first, height = self.rows_at(sub)
        return pltpu.make_async_remote_copy(
            self.kept[group].at[self.own(group, self.source(step, part), first, height)],
            self.box[group].at[self.taken(group, step, part, first, height)],
            r.ring_send.at[group, part, sub, step], r.ring_recv.at[group, part, sub, step],
            device_id=self.targets[part], device_id_type=MESH,
        )

    def here_sum(self, group, ring, first, height):
        value = self.kept[group][self.own(group, ring, first, height)].astype(F32)
        return value + self.box[group][self.theirs(group, ring, first, height)].astype(F32)

    def advance(self, group, step, part, sub, fresh=False):
        if not fresh:
            self.onward(group, step - 1, part, sub).wait_recv()
        ring = self.source(step, part)

        def add(first, height):
            value = self.here_sum(group, ring, first, height)
            if not fresh:
                value = value + self.box[group][self.taken(group, step - 1, part, first, height)].astype(F32)
            self.kept[group][self.own(group, ring, first, height)] = value.astype(BF16)

        self.in_pieces(sub, add)
        self.onward(group, step, part, sub).start()

    def in_pieces(self, sub, body):
        start, height = self.rows_at(sub)

        @pl.loop(0, height // 16)
        def _(k):
            body(pl.multiple_of(start + 16 * k, 16), 16)

    def begin(self, group):
        @pl.loop(0, self.here.chips)
        def _(ring):
            pltpu.make_async_remote_copy(
                self.kept[group].at[self.own(group, ring, 0, self.depth)],
                self.box[group].at[self.theirs(group, ring, 0, self.depth)],
                self.r.over_send.at[group, ring], self.r.over_recv.at[group, ring], device_id=self.sibling, device_id_type=MESH,
            ).wait_recv()

        for part in range(2):
            self.advance(group, 0, part, part, True)
        for part in range(2):
            self.advance(group, 1, part, 1 - part, True)
        if group == ATTN:
            self.small_across().wait_recv()
            self.small_advance(0, 0, True)
            self.small_advance(1, 1, True)

    def tick(self, group, n):
        step, leads = (n + 1) // 2 + 1, n % 2
        for part in range(2):
            self.advance(group, step, part, 1 - part if leads else part)
        if group == ATTN and not leads:
            self.small_advance(step, 0)
            if step > 1:
                self.small_advance(step, 1)

    def sends_done(self, group):
        for part in range(2):
            self.onward(group, 0, part, part).wait_send()
            for step in range(1, self.hops):
                for sub in range(2):
                    self.onward(group, step, part, sub).wait_send()

    def rest(self, group):
        self.end(group)
        for group in (ATTN, CROSS, INNER, OUTER):
            self.sends_done(group)

    def end(self, group):
        r, last = self.r, self.hops - 1
        for sub in range(2):
            for part in range(2):
                self.onward(group, last, part, sub).wait_recv()
            target = r.inner_out if group == INNER else r.total

            def add(first, height):
                value = self.here_sum(group, self.here.ring, first, height)
                for part in range(2):
                    value = value + self.box[group][self.taken(group, last, part, first, height)].astype(F32)
                target[pl.ds(first, height), 0 : self.box[group].shape[2]] = value

            self.in_pieces(sub, add)
        block = r.value_w.shape[1]
        if group == ATTN:
            r.pair_out[1] = r.total[:, 0:block]
            r.value_out[...] = r.total[:, block : 2 * block]
            r.pair_out[0] = r.total[:, 2 * block : 3 * block]
            r.out_out[...] = r.total[:, 3 * block : 4 * block].T
            at = self.small_at(self.here.ring)
            value = r.small[at] + r.small_theirs[at]
            for part in range(2):
                self.small_onward(last, part).wait_recv()
                value = value + r.small_taken[part, last]
            r.tiny_out[...] = value
        if group == CROSS:
            r.first_out[...] = r.total[:, 0:block]
            r.second_out[...] = r.total[:, block : 2 * block]
        if group == OUTER:
            r.outer_out[...] = r.total[...]


    def small_at(self, ring):
        line, at = self.here.at(ring)
        return at, line * CORES + self.here.core

    def small_across(self):
        r = self.r
        return pltpu.make_async_remote_copy(
            r.small, r.small_theirs, r.small_sem.at[0], r.small_sem.at[1], device_id=self.sibling, device_id_type=MESH
        )

    def small_onward(self, step, part):
        r = self.r
        return pltpu.make_async_remote_copy(
            r.small_sent.at[part, step], r.small_taken.at[part, step], r.tiny_send.at[part, step], r.tiny_recv.at[part, step],
            device_id=self.targets[part], device_id_type=MESH,
        )

    def small_advance(self, step, part, fresh=False):
        at = self.small_at(self.source(step, part))
        value = self.r.small[at] + self.r.small_theirs[at]
        if not fresh:
            self.small_onward(step - 1, part).wait_recv()
            value = value + self.r.small_taken[part, step - 1]
        self.r.small_sent[part, step] = value
        self.small_onward(step, part).start()

    def small_begin(self):
        r, depth = self.r, self.depth
        r.small[...] = jnp.zeros_like(r.small)
        kinds = r.onehot.shape[0] // self.dp
        heads_at = self.heads_at
        for tt in range(self.tensor):
            for d in range(self.dp):
                r.small[tt, d, 0:3, 0:depth] = r.gains_out[0:3, d * depth : (d + 1) * depth]
                r.small[tt, d, 3 : 3 + heads_at, 0:kinds] = r.bias_out[
                    8 * tt : 8 * tt + heads_at, d * kinds : (d + 1) * kinds
                ]
        self.small_across().start()


    def home_copy(self, k):
        r, here, tensor = self.r, self.here, self.tensor
        nrow, half, places = r.home_in.shape[0], tensor // 2, r.home_in.shape[2]
        place = here.pipe * (here.core * half + k % half) + (1 - here.pipe) * k
        which = here.pipe * (k // half) + (1 - here.pipe) * here.core
        owner = lax.div(here.t, nrow)
        source = r.rows_out.at[pl.ds(k * places, places)]
        slot = r.home_in.at[lax.rem(here.t, nrow), which]
        recv = r.home_recv.at[lax.rem(here.t, nrow), which]
        return (
            jnp.logical_and(place == here.t, owner == here.core),
            lambda: pltpu.make_async_copy(source, slot, recv),
            lambda: pltpu.make_async_remote_copy(
                source, slot, r.home_send.at[k], recv,
                device_id={"dp": here.group * CORES + owner, "tensor": place}, device_id_type=MESH,
            ),
        )

    def home(self):
        for k in range(self.tensor):
            stays, inside, away = self.home_copy(k)

            @pl.when(stays)
            def _():
                inside().start()

            @pl.when(jnp.logical_not(stays))
            def _():
                away().start()

    def home_done(self, unused=None):
        r = self.r
        places = r.home_in.shape[2]
        for i in range(r.home_in.shape[0]):
            for which in range(2):
                pltpu.make_async_copy(
                    r.rows_out.at[pl.ds(0, places)], r.home_in.at[i, which], r.home_recv.at[i, which]
                ).wait()
                r.home_out[i, which] = r.home_in[i, which].astype(F32)

    def close(self):
        r = self.r
        for k in range(self.tensor):
            stays, inside, away = self.home_copy(k)

            @pl.when(jnp.logical_not(stays))
            def _():
                away().wait_send()

        self.small_across().wait_send()

        for part in range(2):
            for step in range(part, self.hops):
                self.small_onward(step, part).wait_send()


def fits_fused(tensor, dp, depth, units, width):
    chips = tensor * dp // CORES
    return (
        depth % 32 == 0
        and 4 * depth <= width
        and chips <= 2 * tensor
        and chips == 2 * tensor == 8
        and units == width == 6 * LANES
    )


def fused_kernel(tensor, dp, heads_at, names, *refs):
    here = Place(tensor, dp)
    r = types.SimpleNamespace(**dict(zip(names, refs)))
    line = [
        {"dp": here.group * CORES + lax.rem(here.core + j, CORES), "tensor": lax.rem(here.t + k, tensor)}
        for j in range(CORES)
        for k in range(tensor)
        if j + k > 0
    ]
    across = [{"pipe": 1 - here.pipe, "dp": here.group * CORES + k} for k in range(CORES)]
    meet([here.neighbour(1), here.neighbour(-1)] + line + across)
    supply, drain = Rings(r, here, tensor, dp), Sums(r, here, tensor, dp)
    drain.heads_at = heads_at
    work(r, here, supply, drain, tensor, heads_at)


def fused(tensor, dp, rows, enc_lengths, dec_lengths, gains, bias, buckets, weights):
    nrow, two, places, width = rows.shape
    depth, block = weights[1].shape
    units = weights[5].shape[1]
    heads_at, _, kinds = bias.shape
    chips = tensor * dp // CORES
    wide = -(-max(depth, kinds // dp) // LANES) * LANES
    sems = pltpu.SemaphoreType.DMA
    scratch = arrays(tensor, heads_at, places, width, units, buckets.shape[1], kinds)
    scratch.update(
        lengths_in=held(8, LANES, dtype=jnp.int32),
        table_in=held(8, LANES, dtype=F32),
        lengths=held(CORES, 8, LANES, dtype=jnp.int32),
        tables=held(tensor, 8, LANES, dtype=F32),
        own_cross=held(chips, depth, 2 * block),
        own_outer=held(chips, depth, units),
        own_inner=held(chips, depth, units),
        total=held(depth, units, dtype=F32),
        rows_out=held(tensor * places, width),
        gains_out=held(8, width, dtype=F32),
        bias_out=held(8 * tensor, LANES, dtype=F32),
        home_in=held(nrow, two, places, width),
        small=held(tensor, dp, 8, wide, dtype=F32),
        small_theirs=held(tensor, dp, 8, wide, dtype=F32),
        small_sent=held(2, chips // 2, 8, wide, dtype=F32),
        small_taken=held(2, chips // 2, 8, wide, dtype=F32),
        block_send=sems((nrow,)), block_recv=sems((tensor,)), pass_send=sems((tensor,)), pass_recv=sems((tensor,)),
        local_sem=sems((3,)), small_send=sems((tensor,)), small_recv=sems((tensor,)), own_sem=sems((4,)),
        ring_send=sems((4, 2, 2, chips // 2)), ring_recv=sems((4, 2, 2, chips // 2)),
        over_send=sems((4, chips)), over_recv=sems((4, chips)), kept_sem=sems((2, dp // CORES)),
        small_sem=sems((2,)), tiny_send=sems((2, chips // 2)), tiny_recv=sems((2, chips // 2)),
        home_send=sems((tensor,)), home_recv=sems((nrow, two)),
        free_sem=pltpu.SemaphoreType.REGULAR((3,)),
    )
    inputs = ["rows", "enc_lengths", "dec_lengths", "gains", "bias_w", "buckets"]
    inputs += ["query_key_w", "value_w", "out_w", "first_w", "second_w", "inner_w", "outer_w"]
    outputs = dict(
        home_out=rows.shape, tiny_out=(8, wide), pair_out=(2, depth, block), value_out=(depth, block),
        out_out=(block, depth), first_out=(depth, block), second_out=(depth, block), inner_out=(depth, units),
        outer_out=(depth, units),
    )
    return pl.pallas_call(
        functools.partial(fused_kernel, tensor, dp, heads_at, inputs + list(outputs) + list(scratch)),
        out_shape=tuple(jax.ShapeDtypeStruct(shape, F32) for shape in outputs.values()),
        in_specs=[ANY] + [VMEM] * 12,
        out_specs=(VMEM,) * len(outputs),
        scratch_shapes=list(scratch.values()),
        compiler_params=pltpu.CompilerParams(collective_id=3, has_side_effects=True, vmem_limit_bytes=VMEM_LIMIT),
        name="fused",
    )(rows, enc_lengths, dec_lengths, gains, bias, buckets, *weights)


def pad_to(array, *shape):
    return jnp.pad(array, [(0, full - have) for full, have in zip(shape, array.shape)])


def shards(
    tensor, dp, section_rows, enc_lengths, dec_lengths, enc_buckets, dec_buckets, norm_gains, rel_bias,
    query_key_w, value_w, attn_out_w, cross_first, cross_second, ff_in, ff_out,
):
    depth = value_w.shape[1]
    width = section_rows.shape[-1]
    on_encoder = lax.axis_index("pipe") == 0
    ranges = -(-enc_buckets.shape[0] // LANES) * LANES
    dec_all = jnp.concatenate([jnp.zeros((dec_buckets.shape[0] - 1,), jnp.int32), dec_buckets])
    bucket_row = jnp.where(on_encoder, pad_to(enc_buckets, ranges), pad_to(dec_all, ranges))[None]
    gains = norm_gains.transpose(1, 0, 2)
    bias = rel_bias.transpose(2, 0, 1)
    weights = (query_key_w[0], value_w[0], attn_out_w[0], cross_first[0], cross_second[0], ff_in[0], ff_out[0].T)
    run = fused if fits_fused(tensor, dp, depth, ff_in.shape[2], width) else in_three
    home, tiny, *grads, outer = run(
        tensor, dp, section_rows[0], enc_lengths, dec_lengths, gains, bias, bucket_row, weights
    )
    if run is fused:
        home, tiny, *grads, outer = copied(home, tiny, *grads, outer)
    heads_at, kinds = bias.shape[0], bias.shape[2] // dp
    return (
        (home[None], tiny[:3, :depth][None], tiny[3 : 3 + heads_at, :kinds].T[None])
        + tuple(grad[None] for grad in grads)
        + (outer.T[None],)
    )


def copied(*results):
    def kernel(*refs):
        for source, target in zip(refs[: len(results)], refs[len(results) :]):
            target[...] = source[...]

    return pl.pallas_call(
        kernel,
        out_shape=tuple(jax.ShapeDtypeStruct(result.shape, result.dtype) for result in results),
        in_specs=[VMEM] * len(results),
        out_specs=(VMEM,) * len(results),
        name="copied",
    )(*results)


def in_three(tensor, dp, section_rows, enc_lengths, dec_lengths, gains, bias, buckets, weights):
    query_key, value, out, first, second, inner, outer = weights
    nrow, _, _, width = section_rows.shape
    heads_at, _, kinds = bias.shape
    lengths = pad_to(jnp.concatenate([enc_lengths, dec_lengths], axis=0), 8, LANES)
    table = pad_to(bias[:, 0], 8, LANES)
    depth, block = value.shape
    units = inner.shape[1]
    pack = jnp.concatenate([query_key[1], value, query_key[0], out.T, first, second, inner, outer], axis=1)
    rows, gathered, lengths, tables = gather(tensor, dp, section_rows, pack, lengths, table)
    grads, finished, gain_grads, bias = blocks(
        tensor, dp, heads_at, kinds, rows, gathered.reshape(tensor, width, -1), gains, lengths, tables, buckets
    )
    held_kinds = kinds // dp
    wide = -(-max(depth, held_kinds) // LANES) * LANES
    gain_part = pad_to(gain_grads[:3].reshape(3, dp, depth).transpose(1, 0, 2), dp, 3, wide)
    bias_part = bias.reshape(tensor, 8, LANES)[:, :heads_at, :kinds].reshape(tensor, heads_at, dp, held_kinds)
    bias_part = pad_to(bias_part.transpose(0, 2, 1, 3), tensor, dp, 5, wide)
    small = jnp.concatenate([jnp.broadcast_to(gain_part[None], (tensor,) + gain_part.shape), bias_part], axis=2)
    total, tiny, home = scatter(
        tensor, dp, grads.reshape(tensor, dp, depth, -1), small, finished.reshape(tensor, -1, width), nrow
    )
    key, value, query, out, first, second = [total[:, k * block : (k + 1) * block] for k in range(6)]
    inner, outer = total[:, 6 * block : 6 * block + units], total[:, 6 * block + units :]
    return (
        home.astype(F32), tiny,
        jnp.stack([query, key]), value, out.T, first, second, inner, outer,
    )


def solution(mesh):
    sizes = dict(mesh.shape)
    return jax.shard_map(
        functools.partial(shards, sizes["tensor"], sizes["dp"]),
        mesh=mesh,
        in_specs=(
            P("pipe", "dp", None, "tensor", None),
            P("dp", None),
            P("dp", None),
            P(),
            P(),
            P("pipe", None, None),
            P("pipe", None, "tensor"),
            P("pipe", None, "dp", "tensor"),
            P("pipe", "dp", "tensor"),
            P("pipe", "tensor", "dp"),
            P("pipe", "dp", "tensor"),
            P("pipe", "dp", "tensor"),
            P("pipe", "dp", "tensor"),
            P("pipe", "tensor", "dp"),
        ),
        out_specs=(
            P("pipe", "dp", None, "tensor", None),
            P("pipe", None, "dp"),
            P("pipe", "dp", "tensor"),
            P("pipe", None, "dp", "tensor"),
            P("pipe", "dp", "tensor"),
            P("pipe", "tensor", "dp"),
            P("pipe", "dp", "tensor"),
            P("pipe", "dp", "tensor"),
            P("pipe", "dp", "tensor"),
            P("pipe", "tensor", "dp"),
        ),
        check_vma=False,
    )
```

profile of v0, /device:TPU:8, one launch (start us, length us, event | category | flops | bytes accessed | tf_op | source)
XLA Modules:
  0.0 234.2 jit_solution(401172809763016095)
XLA Ops:
  0.6 0.0 copy-start.1
  0.7 0.0 copy-start.2
  0.7 0.7 copy-done.1
  1.3 0.0 copy-done.2
  1.3 0.7 pad_select_fusion
  2.0 226.7 %fused.1 = (f32[2,2,64,768]{3,2,1,0:T(8,128)}, f32[8,256]{1,0:T(8,128)}, f32[2,192,192]{2,1,0:T(8,128)}, f32[192,192]{1,0:T(8,128)}, f32[192,192]{1,0:T(8,128)},...) custom-call(bf16[2,2,64,768]{3,2,1,0:T(8,128)(2,1)} %bitcast.29, ...), custom_call_target="tpu_custom_call" | custom-call | tf_op jit(solution)/shard_map/fused/pallas_call | solution.py:1868
  228.7 3.6 %copied.1 = (f32[2,2,64,768]{3,2,1,0:T(8,128)}, f32[8,256]{1,0:T(8,128)}, f32[2,192,192]{2,1,0:T(8,128)}, f32[192,192]{1,0:T(8,128)}, f32[192,192]{1,0:T(8,128)}...) custom-call(f32[2,2,64,768]{3,2,1,0:T(8,128)} %get-tuple-element.28.refs_0_, ...), custom_call_target="tpu_custom_call" | custom-call | tf_op jit(solution)/shard_map/copied/pallas_call | solution.py:1915
  232.3 0.0 copy-start
  232.3 0.7 copy-done
  233.0 0.6 copy.24
  233.6 0.6 copy.25
  (2 shorter events, 0.0 us)
Async XLA Ops:
  0.6 0.7 copy-start.1
  0.7 0.7 copy-start.2
  232.3 0.7 copy-start
where the time goes:
time: 234 us
  Pallas kernels  230 us (98%)
  local copies, waits for them, and re-layouts  2.53 us (1%)
    pallas_call x1, Pallas kernels, fused(): pl.pallas_call(functools.partial(fused_kernel, tensor, dp, heads_at, inpu...  227 us

commit v1 on v0

--- a/solution.py
+++ b/solution.py
@@ -485,7 +485,7 @@
     return lax.rsqrt(jnp.mean(value * value, axis=-1, keepdims=True) + EPSILON)
 
 
-def in_rows(count, body, piece=32):
+def in_rows(count, body, piece=128):
     @pl.loop(0, count // piece)
     def _(k):
         body(pl.ds(pl.multiple_of(k * piece, piece), piece))
@@ -654,6 +654,17 @@
         return (head // heads_at) * 8 + lax.rem(head, heads_at)
 
     def bias_vectors():
+        enc, dec = r.enc_buckets.shape[1], r.dec_buckets.shape[1]
+        r.buckets[...] = jnp.zeros_like(r.buckets)
+
+        @pl.when(here.pipe == 0)
+        def _():
+            r.buckets[0:1, 0:enc] = r.enc_buckets[...]
+
+        @pl.when(here.pipe == 1)
+        def _():
+            r.buckets[0:1, dec - 1 : 2 * dec - 1] = r.dec_buckets[...]
+
         buckets = lax.broadcasted_iota(jnp.int32, r.onehot.shape, 0) == r.buckets[0:1, :]
         r.onehot[...] = buckets.astype(F32)
         for tt in range(tensor):
@@ -1010,9 +1021,9 @@
             drain.home()
 
         steps = schedule(
-            [("tick", CROSS, 4), ("begin", INNER), ("tick", OUTER, 1)], [("end", CROSS), ("tick", OUTER, 2)],
-            [], [("tick", INNER, 0)], [], [],
-            [], [], [("tick", INNER, 1)], [], [("tick", OUTER, 3), ("tick", OUTER, 4)], [],
+            [("tick", CROSS, 4), ("begin", INNER)], [("tick", OUTER, 1)],
+            [], [("end", CROSS)], [], [("tick", OUTER, 2)],
+            [("tick", INNER, 0)], [], [("tick", INNER, 1)], [], [("tick", OUTER, 3)], [("tick", OUTER, 4)],
             [("tick", INNER, 2), ("tick", ATTN, 0), ("end", OUTER), ("tick", INNER, 3), ("tick", ATTN, 1), ("tick", ATTN, 2)]
             + [("home_done", None), ("tick", INNER, 4), ("tick", ATTN, 3), ("tick", ATTN, 4), ("end", INNER)],
         )
@@ -1077,10 +1088,12 @@
         to_bf16(r.d_resid, r.branch, rows)
         tells = []
         for pair in range(pairs_here):
+            at = pair_lanes(pair)
+            firsts = [k * half_width + pair * LANES for k in range(CORES)]
+            both = jnp.concatenate([r.square[SECOND, :, first : first + LANES] for first in firsts], axis=1)
+            value = nn(r.branch[0:rows, :], both).astype(BF16)
             for k in range(CORES):
-                at = pair_lanes(pair)
-                first = k * half_width + pair * LANES
-                r.send_back[k, :, at] = nn(r.branch[0:rows, :], r.square[SECOND, :, first : first + LANES]).astype(BF16)
+                r.send_back[k, :, at] = value[:, k * LANES : (k + 1) * LANES]
                 tells.append(
                     pltpu.make_async_remote_copy(
                         r.send_back.at[k, :, at], r.cross_back.at[pl.ds(pl.multiple_of(c * rows, rows), rows), at],
@@ -1183,6 +1196,7 @@
         vectors=held(8 * tensor, ranges, dtype=F32),
         diagonals=held(8 * tensor, ranges, dtype=F32),
         onehot=held(kinds, ranges, dtype=F32),
+        buckets=held(8, ranges, dtype=jnp.int32),
         gain_parts=held(8, width, dtype=F32),
         send_sem=pltpu.SemaphoreType.DMA((14,)),
         recv_sem=pltpu.SemaphoreType.DMA((14,)),
@@ -1261,10 +1275,11 @@
     places, width = rows.shape[2:]
     units = (weights.shape[2] - 6 * (width // tensor)) // 2
     half_rows = tensor * places
-    scratch = arrays(tensor, heads_at, places, width, units, buckets.shape[1], kinds)
+    ranges = -(-buckets[0].shape[1] // LANES) * LANES
+    scratch = arrays(tensor, heads_at, places, width, units, ranges, kinds)
     scratch["load_sem"] = pltpu.SemaphoreType.DMA((5, tensor))
     scratch["stage_sem"] = pltpu.SemaphoreType.DMA((2,))
-    names = ["x_hbm", "w_hbm", "gains", "lengths", "tables", "buckets", "grads_hbm", "rows_out", "gains_out", "bias_out"]
+    names = ["x_hbm", "w_hbm", "gains", "lengths", "tables", "enc_buckets", "dec_buckets", "grads_hbm", "rows_out", "gains_out", "bias_out"]
     return pl.pallas_call(
         functools.partial(blocks_kernel, tensor, dp, heads_at, names + list(scratch)),
         out_shape=(
@@ -1273,12 +1288,28 @@
             jax.ShapeDtypeStruct((8, width), F32),
             jax.ShapeDtypeStruct((8 * tensor, LANES), F32),
         ),
-        in_specs=[ANY, ANY] + [VMEM] * 4,
+        in_specs=[ANY, ANY] + [VMEM] * 5,
         out_specs=(ANY, VMEM, VMEM, VMEM),
         scratch_shapes=list(scratch.values()),
         compiler_params=pltpu.CompilerParams(collective_id=2, has_side_effects=True, vmem_limit_bytes=VMEM_LIMIT),
         name="blocks",
-    )(rows, weights, gains, lengths, tables, buckets)
+    )(rows, weights, gains, lengths, tables, *buckets)
+
+
+def all_sends(r, box, group, depth, hops, targets):
+    for part in range(2):
+        sent = box.at[0, pl.ds(0, (2 * hops - 1) * depth // 2), :]
+        pltpu.make_async_remote_copy(
+            sent, sent, r.ring_send.at[group, part], r.ring_recv.at[group, part, 0, 0],
+            device_id=targets[part], device_id_type=MESH,
+        ).wait_send()
+
+
+def all_over(r, box, group, here, depth):
+    whole = box.at[pl.ds(0, here.chips * depth // box.shape[1])]
+    return pltpu.make_async_remote_copy(
+        whole, whole, r.over_send.at[group], r.over_recv.at[group], device_id=here.sibling(), device_id_type=MESH
+    )
 
 
 class Rings:
@@ -1378,7 +1409,7 @@
         slot = target.at[at, pl.ds(pl.multiple_of(first + half * sub, 16), half), :]
         packed = r.stage.at[0, pl.ds(group * self.depth + half * sub, half), pl.ds(0, target.shape[2])]
         return pltpu.make_async_remote_copy(
-            packed if step == 0 else slot, slot, r.ring_send.at[group, part, sub, step], r.ring_recv.at[group, part, sub, step],
+            packed if step == 0 else slot, slot, r.ring_send.at[group, part], r.ring_recv.at[group, part, sub, step],
             device_id=self.targets[part], device_id_type=MESH,
         )
 
@@ -1389,7 +1420,7 @@
         slot = target.at[at, pl.ds(first, self.depth), :]
         packed = r.stage.at[0, pl.ds(group * self.depth, self.depth), pl.ds(0, target.shape[2])]
         return pltpu.make_async_remote_copy(
-            packed if first_time else slot, slot, r.over_send.at[group, ring], r.over_recv.at[group, ring],
+            packed if first_time else slot, slot, r.over_send.at[group], r.over_recv.at[group],
             device_id=self.sibling, device_id_type=MESH,
         )
 
@@ -1423,21 +1454,24 @@
                 self.over(group, self.ring_at(step, part)).start()
 
     def sends_done(self, group):
-        for part in range(2):
-            for sub in range(2):
-                for step in range(self.hops):
-                    if step < self.hops - 1 or sub == part:
-                        self.onward(group, step, part, sub).wait_send()
+        all_sends(self.r, self.landing[group], group, self.depth, self.hops, self.targets)
 
     def finish(self, group):
-        @pl.loop(0, self.here.chips)
-        def _(ring):
-            self.over(group, ring).wait_recv()
-
+        all_over(self.r, self.landing[group], group, self.here, self.depth).wait_recv()
         self.own(group).wait()
 
     def start(self):
         r, depth = self.r, self.depth
+        block = r.value_w.shape[1]
+
+        def band(group, pieces):
+            wide = pieces[0].shape[1]
+            for k, piece in enumerate(pieces):
+                r.stage[0, group * depth : (group + 1) * depth, k * wide : (k + 1) * wide] = piece
+
+        band(ATTN, [r.query_key_w[1], r.value_w[...], r.query_key_w[0], r.out_w[...].T])
+        self.order(ATTN)
+        self.begin(ATTN)
         nrow = r.rows.shape[0]
         r.lengths_in[...] = jnp.zeros_like(r.lengths_in)
         r.lengths_in[0:nrow, 0 : r.enc_lengths.shape[1]] = r.enc_lengths[...]
@@ -1449,16 +1483,6 @@
             lambda i: (self.block_kept(i).start(), self.block_pass(r.rows.at[i], self.here.t).start()),
             lambda i: self.block_out(i).start(),
         )
-        block = r.value_w.shape[1]
-
-        def band(group, pieces):
-            wide = pieces[0].shape[1]
-            for k, piece in enumerate(pieces):
-                r.stage[0, group * depth : (group + 1) * depth, k * wide : (k + 1) * wide] = piece
-
-        band(ATTN, [r.query_key_w[1], r.value_w[...], r.query_key_w[0], r.out_w[...].T])
-        self.order(ATTN)
-        self.begin(ATTN)
         for copy in self.small_copies():
             copy.start()
         band(INNER, [r.inner_w[...]])
@@ -1504,10 +1528,7 @@
 
         for group in self.groups:
             self.sends_done(group)
-
-            @pl.loop(0, self.here.chips)
-            def _(ring):
-                self.over(group, ring).wait_send()
+            all_over(r, self.landing[group], group, self.here, self.depth).wait_send()
 
 
 class Sums:
@@ -1569,7 +1590,7 @@
             made.append(
                 pltpu.make_async_remote_copy(
                     rows_of(1 - self.here.core), self.box[group].at[self.theirs(group, ring, 0, depth)],
-                    r.over_send.at[group, ring], r.over_recv.at[group, ring], device_id=self.sibling, device_id_type=MESH,
+                    r.pair_send.at[slot, line], r.over_recv.at[group], device_id=self.sibling, device_id_type=MESH,
                 )
             )
         return made
@@ -1600,7 +1621,7 @@
         return pltpu.make_async_remote_copy(
             self.kept[group].at[self.own(group, self.source(step, part), first, height)],
             self.box[group].at[self.taken(group, step, part, first, height)],
-            r.ring_send.at[group, part, sub, step], r.ring_recv.at[group, part, sub, step],
+            r.ring_send.at[group, part], r.ring_recv.at[group, part, sub, step],
             device_id=self.targets[part], device_id_type=MESH,
         )
 
@@ -1630,14 +1651,7 @@
             body(pl.multiple_of(start + 16 * k, 16), 16)
 
     def begin(self, group):
-        @pl.loop(0, self.here.chips)
-        def _(ring):
-            pltpu.make_async_remote_copy(
-                self.kept[group].at[self.own(group, ring, 0, self.depth)],
-                self.box[group].at[self.theirs(group, ring, 0, self.depth)],
-                self.r.over_send.at[group, ring], self.r.over_recv.at[group, ring], device_id=self.sibling, device_id_type=MESH,
-            ).wait_recv()
-
+        all_over(self.r, self.box[group], group, self.here, self.depth).wait_recv()
         for part in range(2):
             self.advance(group, 0, part, part, True)
         for part in range(2):
@@ -1657,11 +1671,7 @@
                 self.small_advance(step, 1)
 
     def sends_done(self, group):
-        for part in range(2):
-            self.onward(group, 0, part, part).wait_send()
-            for step in range(1, self.hops):
-                for sub in range(2):
-                    self.onward(group, step, part, sub).wait_send()
+        all_sends(self.r, self.box[group], group, self.depth, self.hops, self.targets)
 
     def rest(self, group):
         self.end(group)
@@ -1683,6 +1693,7 @@
 
             self.in_pieces(sub, add)
         block = r.value_w.shape[1]
+        done = {ATTN: ("pair_out", "value_out", "out_out", "tiny_out"), CROSS: ("first_out", "second_out")}
         if group == ATTN:
             r.pair_out[1] = r.total[:, 0:block]
             r.value_out[...] = r.total[:, block : 2 * block]
@@ -1699,6 +1710,12 @@
             r.second_out[...] = r.total[:, block : 2 * block]
         if group == OUTER:
             r.outer_out[...] = r.total[...]
+        for name in done.get(group, ("inner_out",) if group == INNER else ("outer_out",)):
+            self.result(name).start()
+
+    def result(self, name):
+        r = self.r
+        return pltpu.make_async_copy(getattr(r, name), getattr(r, name + "_hbm"), r.result_sem.at[r.results.index(name)])
 
 
     def small_at(self, ring):
@@ -1780,6 +1797,7 @@
                     r.rows_out.at[pl.ds(0, places)], r.home_in.at[i, which], r.home_recv.at[i, which]
                 ).wait()
                 r.home_out[i, which] = r.home_in[i, which].astype(F32)
+        self.result("home_out").start()
 
     def close(self):
         r = self.r
@@ -1790,6 +1808,8 @@
             def _():
                 away().wait_send()
 
+        for name in r.results:
+            self.result(name).wait()
         self.small_across().wait_send()
 
         for part in range(2):
@@ -1804,11 +1824,12 @@
         and 4 * depth <= width
         and chips <= 2 * tensor
         and chips == 2 * tensor == 8
+        and chips * depth == 2 * width
         and units == width == 6 * LANES
     )
 
 
-def fused_kernel(tensor, dp, heads_at, names, *refs):
+def fused_kernel(tensor, dp, heads_at, results, names, *refs):
     here = Place(tensor, dp)
     r = types.SimpleNamespace(**dict(zip(names, refs)))
     line = [
@@ -1818,7 +1839,16 @@
         if j + k > 0
     ]
     across = [{"pipe": 1 - here.pipe, "dp": here.group * CORES + k} for k in range(CORES)]
+    r.results = results
+    given = [name for name in names if name + "_hbm" in names and name not in results]
+    copies = [
+        pltpu.make_async_copy(getattr(r, name + "_hbm"), getattr(r, name), r.given_sem.at[k]) for k, name in enumerate(given)
+    ]
+    for copy in copies:
+        copy.start()
     meet([here.neighbour(1), here.neighbour(-1)] + line + across)
+    for copy in copies:
+        copy.wait()
     supply, drain = Rings(r, here, tensor, dp), Sums(r, here, tensor, dp)
     drain.heads_at = heads_at
     work(r, here, supply, drain, tensor, heads_at)
@@ -1832,7 +1862,13 @@
     chips = tensor * dp // CORES
     wide = -(-max(depth, kinds // dp) // LANES) * LANES
     sems = pltpu.SemaphoreType.DMA
-    scratch = arrays(tensor, heads_at, places, width, units, buckets.shape[1], kinds)
+    ranges = -(-buckets[0].shape[1] // LANES) * LANES
+    scratch = arrays(tensor, heads_at, places, width, units, ranges, kinds)
+    given = dict(enc_lengths=enc_lengths, dec_lengths=dec_lengths, gains=gains, bias_w=bias)
+    given.update(enc_buckets=buckets[0], dec_buckets=buckets[1])
+    names = ("query_key_w", "value_w", "out_w", "first_w", "second_w", "inner_w", "outer_w")
+    given.update(zip(names, weights))
+    scratch.update({name: pltpu.VMEM(array.shape, array.dtype) for name, array in given.items()})
     scratch.update(
         lengths_in=held(8, LANES, dtype=jnp.int32),
         table_in=held(8, LANES, dtype=F32),
@@ -1852,28 +1888,29 @@
         small_taken=held(2, chips // 2, 8, wide, dtype=F32),
         block_send=sems((nrow,)), block_recv=sems((tensor,)), pass_send=sems((tensor,)), pass_recv=sems((tensor,)),
         local_sem=sems((3,)), small_send=sems((tensor,)), small_recv=sems((tensor,)), own_sem=sems((4,)),
-        ring_send=sems((4, 2, 2, chips // 2)), ring_recv=sems((4, 2, 2, chips // 2)),
-        over_send=sems((4, chips)), over_recv=sems((4, chips)), kept_sem=sems((2, dp // CORES)),
+        ring_send=sems((4, 2)), ring_recv=sems((4, 2, 2, chips // 2)),
+        over_send=sems((4,)), over_recv=sems((4,)), kept_sem=sems((2, dp // CORES)), pair_send=sems((2, dp // CORES)),
         small_sem=sems((2,)), tiny_send=sems((2, chips // 2)), tiny_recv=sems((2, chips // 2)),
         home_send=sems((tensor,)), home_recv=sems((nrow, two)),
-        free_sem=pltpu.SemaphoreType.REGULAR((3,)),
+        free_sem=pltpu.SemaphoreType.REGULAR((3,)), given_sem=sems((len(given),)),
     )
-    inputs = ["rows", "enc_lengths", "dec_lengths", "gains", "bias_w", "buckets"]
-    inputs += ["query_key_w", "value_w", "out_w", "first_w", "second_w", "inner_w", "outer_w"]
+    inputs = ["rows"] + [name + "_hbm" for name in given]
     outputs = dict(
         home_out=rows.shape, tiny_out=(8, wide), pair_out=(2, depth, block), value_out=(depth, block),
         out_out=(block, depth), first_out=(depth, block), second_out=(depth, block), inner_out=(depth, units),
         outer_out=(depth, units),
     )
+    scratch.update({name: held(*shape, dtype=F32) for name, shape in outputs.items()})
+    scratch["result_sem"] = sems((len(outputs),))
     return pl.pallas_call(
-        functools.partial(fused_kernel, tensor, dp, heads_at, inputs + list(outputs) + list(scratch)),
+        functools.partial(fused_kernel, tensor, dp, heads_at, list(outputs), inputs + [name + "_hbm" for name in outputs] + list(scratch)),
         out_shape=tuple(jax.ShapeDtypeStruct(shape, F32) for shape in outputs.values()),
-        in_specs=[ANY] + [VMEM] * 12,
-        out_specs=(VMEM,) * len(outputs),
+        in_specs=[ANY] * (1 + len(given)),
+        out_specs=(ANY,) * len(outputs),
         scratch_shapes=list(scratch.values()),
         compiler_params=pltpu.CompilerParams(collective_id=3, has_side_effects=True, vmem_limit_bytes=VMEM_LIMIT),
         name="fused",
-    )(rows, enc_lengths, dec_lengths, gains, bias, buckets, *weights)
+    )(rows, *given.values())
 
 
 def pad_to(array, *shape):
@@ -1886,39 +1923,58 @@
 ):
     depth = value_w.shape[1]
     width = section_rows.shape[-1]
-    on_encoder = lax.axis_index("pipe") == 0
-    ranges = -(-enc_buckets.shape[0] // LANES) * LANES
-    dec_all = jnp.concatenate([jnp.zeros((dec_buckets.shape[0] - 1,), jnp.int32), dec_buckets])
-    bucket_row = jnp.where(on_encoder, pad_to(enc_buckets, ranges), pad_to(dec_all, ranges))[None]
+    buckets = (enc_buckets[None], dec_buckets[None])
     gains = norm_gains.transpose(1, 0, 2)
     bias = rel_bias.transpose(2, 0, 1)
     weights = (query_key_w[0], value_w[0], attn_out_w[0], cross_first[0], cross_second[0], ff_in[0], ff_out[0].T)
     run = fused if fits_fused(tensor, dp, depth, ff_in.shape[2], width) else in_three
-    home, tiny, *grads, outer = run(
-        tensor, dp, section_rows[0], enc_lengths, dec_lengths, gains, bias, bucket_row, weights
-    )
-    if run is fused:
-        home, tiny, *grads, outer = copied(home, tiny, *grads, outer)
-    heads_at, kinds = bias.shape[0], bias.shape[2] // dp
+    home, tiny, *grads = run(tensor, dp, section_rows[0], enc_lengths, dec_lengths, gains, bias, buckets, weights)
+    gain, kind, home, *grads, outer = copied(depth, bias.shape[0], bias.shape[2] // dp, tiny, home, *grads)
     return (
-        (home[None], tiny[:3, :depth][None], tiny[3 : 3 + heads_at, :kinds].T[None])
+        (home[None], gain.transpose(1, 0, 2), kind.transpose(1, 2, 0))
         + tuple(grad[None] for grad in grads)
         + (outer.T[None],)
     )
 
 
-def copied(*results):
+def copied(depth, heads_at, kinds, tiny, *results):
+    count = len(results)
+
     def kernel(*refs):
-        for source, target in zip(refs[: len(results)], refs[len(results) :]):
-            target[...] = source[...]
-
+        sources, refs = refs[: count + 1], refs[count + 1 :]
+        targets, refs = refs[: count + 2], refs[count + 2 :]
+        held_here, (tiny_ref, in_sem, out_sem) = refs[: count + 2], refs[count + 2 :]
+        ins = [
+            pltpu.make_async_copy(source, there, in_sem.at[k])
+            for k, (source, there) in enumerate(zip(sources, (tiny_ref,) + tuple(held_here[2:])))
+        ]
+        outs = [pltpu.make_async_copy(there, target, out_sem.at[k]) for k, (there, target) in enumerate(zip(held_here, targets))]
+        for copy in ins:
+            copy.start()
+        for copy, out in zip(ins[1:], outs[2:]):
+            copy.wait()
+            out.start()
+        ins[0].wait()
+        for k in range(3):
+            held_here[0][k] = tiny_ref[k : k + 1, 0:depth]
+        for k in range(heads_at):
+            held_here[1][k] = tiny_ref[3 + k : 4 + k, 0:kinds]
+        outs[0].start()
+        outs[1].start()
+        for out in outs:
+            out.wait()
+
+    shapes = [(3, 1, depth), (heads_at, 1, kinds)] + [result.shape for result in results]
+    sems = pltpu.SemaphoreType.DMA
     return pl.pallas_call(
         kernel,
-        out_shape=tuple(jax.ShapeDtypeStruct(result.shape, result.dtype) for result in results),
-        in_specs=[VMEM] * len(results),
-        out_specs=(VMEM,) * len(results),
+        out_shape=tuple(jax.ShapeDtypeStruct(shape, F32) for shape in shapes),
+        in_specs=[ANY] * (count + 1),
+        out_specs=(ANY,) * (count + 2),
+        scratch_shapes=[held(*shape, dtype=F32) for shape in shapes + [tiny.shape]] + [sems((count + 1,)), sems((count + 2,))],
+        compiler_params=pltpu.CompilerParams(vmem_limit_bytes=VMEM_LIMIT),
         name="copied",
-    )(*results)
+    )(tiny, *results)
 
 
 def in_three(tensor, dp, section_rows, enc_lengths, dec_lengths, gains, bias, buckets, weights):

time: 234 us -> 224 us (0.957)
  Pallas kernels: 230 us -> 223 us
  local copies, waits for them, and re-layouts: 2.53 us -> 0 us
    pallas_call x2, Pallas kernels: 230 us -> 223 us  [the longest x1 220 us: fused(): pl.pallas_call(functools.partial(fused_kernel, tensor, dp, heads_at, list...]
    unnamed x8 -> x0, local copies, waits for them, and re-layouts: 2.52 us -> none
where the time goes in v1:
time: 224 us
  Pallas kernels  223 us (100%)
    pallas_call x1, Pallas kernels, fused(): pl.pallas_call(functools.partial(fused_kernel, tensor, dp, heads_at, list...  220 us

profile of v1, /device:TPU:8, one launch (start us, length us, event | category | flops | bytes accessed | tf_op | source)
XLA Modules:
  0.0 224.3 jit_solution(5663926766796198627)
XLA Ops:
  0.6 220.5 %fused.1 = (f32[2,2,64,768]{3,2,1,0:T(8,128)}, f32[8,256]{1,0:T(8,128)}, f32[2,192,192]{2,1,0:T(8,128)}, f32[192,192]{1,0:T(8,128)}, f32[192,192]{1,0:T(8,128)},...) custom-call(bf16[2,2,64,768]{3,2,1,0:T(8,128)(2,1)} %bitcast.26, ...), custom_call_target="tpu_custom_call" | custom-call | tf_op jit(solution)/shard_map/fused/pallas_call | solution.py:1905
  221.2 3.0 %copied.1 = (f32[3,1,192]{2,1,0:T(1,128)}, f32[3,1,8]{2,1,0:T(1,128)}, f32[2,2,64,768]{3,2,1,0:T(8,128)}, f32[2,192,192]{2,1,0:T(8,128)}, f32[192,192]{1,0:T(8,1...) custom-call(f32[8,256]{1,0:T(8,128)} %get-tuple-element.29.refs_0_, ...), custom_call_target="tpu_custom_call" | custom-call | tf_op jit(solution)/shard_map/copied/pallas_call | solution.py:1969

commit v2 on v1

--- a/solution.py
+++ b/solution.py
@@ -792,20 +792,29 @@
             drain.release(which, tt, tt % 2)
 
     def square_grads(rows, which, products, hook):
+        wide = len(products) * block
+        apart = tensor // 2 * wide <= r.stage.shape[2]
         for k in range(tensor // 2):
+            place = k if apart else 0
             for j, (turned, right) in enumerate(products):
 
                 def body(at):
                     value = nn(turned[at, 0:rows], right[0:rows, 2 * k * block : 2 * (k + 1) * block]).astype(BF16)
                     for slot in range(2):
-                        r.stage[slot, at, j * block : (j + 1) * block] = value[:, slot * block : (slot + 1) * block]
+                        first = place * wide + j * block
+                        r.stage[slot, at, first : first + block] = value[:, slot * block : (slot + 1) * block]
 
                 in_rows(width, body, 256)
             for slot in range(2):
-                drain.emit(which, 2 * k + slot, slot)
+                drain.emit(which, 2 * k + slot, slot, place)
             hook(k)
-            for slot in range(2):
-                drain.release(which, 2 * k + slot, slot)
+            if not apart:
+                for slot in range(2):
+                    drain.release(which, 2 * k + slot, slot)
+        if apart:
+            for k in range(tensor // 2):
+                for slot in range(2):
+                    drain.release(which, 2 * k + slot, slot, k)
 
     def gain_done(which):
         r.gains_out[which : which + 1, :] = jnp.sum(r.gain_parts[...], axis=0, keepdims=True)
@@ -1248,17 +1257,18 @@
         self.columns = group_columns(r.raw_a.shape[2] // 4, r.inner.shape[2])
         self.r, self.grads, self.sems = r, grads_hbm, sems
 
-    def copy(self, group, tt, slot):
+    def copy(self, group, tt, slot, place):
         first, wide = self.columns[group]
         return pltpu.make_async_copy(
-            self.r.stage.at[slot, :, pl.ds(0, wide)], self.grads.at[tt, :, pl.ds(first, wide)], self.sems.at[slot]
-        )
-
-    def emit(self, group, tt, slot):
-        self.copy(group, tt, slot).start()
-
-    def release(self, group, tt, slot):
-        self.copy(group, tt, slot).wait()
+            self.r.stage.at[slot, :, pl.ds(place * wide, wide)], self.grads.at[tt, :, pl.ds(first, wide)],
+            self.sems.at[slot + 2 * place],
+        )
+
+    def emit(self, group, tt, slot, place=0):
+        self.copy(group, tt, slot, place).start()
+
+    def release(self, group, tt, slot, place=0):
+        self.copy(group, tt, slot, place).wait()
 
     order = free = allow = begin = tick = rest = end = home = home_done = small_begin = close = nothing
 
@@ -1278,7 +1288,7 @@
     ranges = -(-buckets[0].shape[1] // LANES) * LANES
     scratch = arrays(tensor, heads_at, places, width, units, ranges, kinds)
     scratch["load_sem"] = pltpu.SemaphoreType.DMA((5, tensor))
-    scratch["stage_sem"] = pltpu.SemaphoreType.DMA((2,))
+    scratch["stage_sem"] = pltpu.SemaphoreType.DMA((4,))
     names = ["x_hbm", "w_hbm", "gains", "lengths", "tables", "enc_buckets", "dec_buckets", "grads_hbm", "rows_out", "gains_out", "bias_out"]
     return pl.pallas_call(
         functools.partial(blocks_kernel, tensor, dp, heads_at, names + list(scratch)),
@@ -1572,35 +1582,36 @@
     def ring_of(self, line, at):
         return line * self.tensor + at + (line % 2) * (self.tensor - 1 - 2 * at)
 
-    def pieces(self, group, tt, slot):
+    def pieces(self, group, tt, slot, place=0):
         r, depth = self.r, self.depth
         wide = self.box[group].shape[2]
+        sem = slot + 2 * place
         made = []
         for line in range(self.here.groups):
             ring = self.ring_of(line, tt)
 
             def rows_of(core):
-                return r.stage.at[slot, pl.ds(pl.multiple_of((line * CORES + core) * depth, 16), depth), pl.ds(0, wide)]
+                return r.stage.at[slot, pl.ds(pl.multiple_of((line * CORES + core) * depth, 16), depth), pl.ds(place * wide, wide)]
 
             made.append(
                 pltpu.make_async_copy(
-                    rows_of(self.here.core), self.kept[group].at[self.own(group, ring, 0, depth)], r.kept_sem.at[slot, line]
+                    rows_of(self.here.core), self.kept[group].at[self.own(group, ring, 0, depth)], r.kept_sem.at[sem, line]
                 )
             )
             made.append(
                 pltpu.make_async_remote_copy(
                     rows_of(1 - self.here.core), self.box[group].at[self.theirs(group, ring, 0, depth)],
-                    r.pair_send.at[slot, line], r.over_recv.at[group], device_id=self.sibling, device_id_type=MESH,
+                    r.pair_send.at[sem, line], r.over_recv.at[group], device_id=self.sibling, device_id_type=MESH,
                 )
             )
         return made
 
-    def emit(self, group, tt, slot):
-        for piece in self.pieces(group, tt, slot):
+    def emit(self, group, tt, slot, place=0):
+        for piece in self.pieces(group, tt, slot, place):
             piece.start()
 
-    def release(self, group, tt, slot):
-        for k, piece in enumerate(self.pieces(group, tt, slot)):
+    def release(self, group, tt, slot, place=0):
+        for k, piece in enumerate(self.pieces(group, tt, slot, place)):
             if k % 2:
                 piece.wait_send()
             else:
@@ -1646,9 +1657,9 @@
     def in_pieces(self, sub, body):
         start, height = self.rows_at(sub)
 
-        @pl.loop(0, height // 16)
+        @pl.loop(0, height // 32)
         def _(k):
-            body(pl.multiple_of(start + 16 * k, 16), 16)
+            body(pl.multiple_of(start + 32 * k, 32), 32)
 
     def begin(self, group):
         all_over(self.r, self.box[group], group, self.here, self.depth).wait_recv()
@@ -1889,7 +1900,7 @@
         block_send=sems((nrow,)), block_recv=sems((tensor,)), pass_send=sems((tensor,)), pass_recv=sems((tensor,)),
         local_sem=sems((3,)), small_send=sems((tensor,)), small_recv=sems((tensor,)), own_sem=sems((4,)),
         ring_send=sems((4, 2)), ring_recv=sems((4, 2, 2, chips // 2)),
-        over_send=sems((4,)), over_recv=sems((4,)), kept_sem=sems((2, dp // CORES)), pair_send=sems((2, dp // CORES)),
+        over_send=sems((4,)), over_recv=sems((4,)), kept_sem=sems((4, dp // CORES)), pair_send=sems((4, dp // CORES)),
         small_sem=sems((2,)), tiny_send=sems((2, chips // 2)), tiny_recv=sems((2, chips // 2)),
         home_send=sems((tensor,)), home_recv=sems((nrow, two)),
         free_sem=pltpu.SemaphoreType.REGULAR((3,)), given_sem=sems((len(given),)),

time: 224 us -> 223 us (level)
  no operation moved by 1% of the time
where the time goes in v2:
time: 223 us
  Pallas kernels  222 us (100%)
    pallas_call x1, Pallas kernels, fused(): pl.pallas_call(functools.partial(fused_kernel, tensor, dp, heads_at, list...  219 us

profile of v2, /device:TPU:8, one launch (start us, length us, event | category | flops | bytes accessed | tf_op | source)
XLA Modules:
  0.0 222.7 jit_solution(13738502777145704498)
XLA Ops:
  0.6 218.8 %fused.1 = (f32[2,2,64,768]{3,2,1,0:T(8,128)}, f32[8,256]{1,0:T(8,128)}, f32[2,192,192]{2,1,0:T(8,128)}, f32[192,192]{1,0:T(8,128)}, f32[192,192]{1,0:T(8,128)},...) custom-call(bf16[2,2,64,768]{3,2,1,0:T(8,128)(2,1)} %bitcast.26, ...), custom_call_target="tpu_custom_call" | custom-call | tf_op jit(solution)/shard_map/fused/pallas_call | solution.py:1916
  219.5 3.0 %copied.1 = (f32[3,1,192]{2,1,0:T(1,128)}, f32[3,1,8]{2,1,0:T(1,128)}, f32[2,2,64,768]{3,2,1,0:T(8,128)}, f32[2,192,192]{2,1,0:T(8,128)}, f32[192,192]{1,0:T(8,1...) custom-call(f32[8,256]{1,0:T(8,128)} %get-tuple-element.29.refs_0_, ...), custom_call_target="tpu_custom_call" | custom-call | tf_op jit(solution)/shard_map/copied/pallas_call | solution.py:1980

commit v3 on v2

--- a/solution.py
+++ b/solution.py
@@ -555,8 +555,8 @@
     return lax.broadcasted_iota(jnp.int32, shape, 1) // HEAD_DIM == part
 
 
-def attend(keys, values, queries, mixture, probs, rows, span, pairs, mask, bias, after):
-    @pl.loop(0, pairs)
+def attend(keys, values, queries, mixture, probs, rows, span, pairs, mask, bias, after, unroll=1):
+    @pl.loop(0, pairs, unroll=unroll)
     def _(pair):
         lanes = pl.ds(pl.multiple_of(pair * LANES, LANES), LANES)
         key, query = keys[0:span, lanes], queries[0:rows, lanes]
@@ -978,7 +978,7 @@
 
         attend(
             r.cross_keys, r.cross_values, r.cross_queries, r.cross_mixture, r.cross_probs, span_d, span, pairs_here,
-            r.mask, None, lambda pair: [mix.start() for mix in mixtures(pair)],
+            r.mask, None, lambda pair: [mix.start() for mix in mixtures(pair)], pairs_here,
         )
         supply.close()
         drain.free(0)

time: 223 us -> 223 us (level)
  no operation moved by 1% of the time
where the time goes in v3:
time: 223 us
  Pallas kernels  222 us (100%)
    pallas_call x1, Pallas kernels, fused(): pl.pallas_call(functools.partial(fused_kernel, tensor, dp, heads_at, list...  219 us

profile of v3, /device:TPU:8, one launch (start us, length us, event | category | flops | bytes accessed | tf_op | source)
XLA Modules:
  0.0 222.6 jit_solution(10369364402014866473)
XLA Ops:
  0.6 218.8 %fused.1 = (f32[2,2,64,768]{3,2,1,0:T(8,128)}, f32[8,256]{1,0:T(8,128)}, f32[2,192,192]{2,1,0:T(8,128)}, f32[192,192]{1,0:T(8,128)}, f32[192,192]{1,0:T(8,128)},...) custom-call(bf16[2,2,64,768]{3,2,1,0:T(8,128)(2,1)} %bitcast.26, ...), custom_call_target="tpu_custom_call" | custom-call | tf_op jit(solution)/shard_map/fused/pallas_call | solution.py:1916
  219.4 3.0 %copied.1 = (f32[3,1,192]{2,1,0:T(1,128)}, f32[3,1,8]{2,1,0:T(1,128)}, f32[2,2,64,768]{3,2,1,0:T(8,128)}, f32[2,192,192]{2,1,0:T(8,128)}, f32[192,192]{1,0:T(8,1...) custom-call(f32[8,256]{1,0:T(8,128)} %get-tuple-element.29.refs_0_, ...), custom_call_target="tpu_custom_call" | custom-call | tf_op jit(solution)/shard_map/copied/pallas_call | solution.py:1980
